TPU v7x, 32 devices: a whole 2x2x4 slice. The times are simulated.
32 devices in a mesh: prow: 4 (over y, core), pcol: 8 (over z, x).
Axes of the slice: x: 2, y: 2, z: 4, core: 2. Of those that a mesh axis runs over, the one named last changes fastest.
Arguments:
- trailing: float32 [8, 4, 128, 4, 8, 128], P(None, 'prow', None, None, 'pcol'), may hold values from -8 to 8, as said below
- reflectors: float32 [8, 4, 128, 256], P(None, 'prow', None, 'pcol'), may hold values from -0.5 to 0.5
- tfactor: float32 [256, 256], replicated, may hold values from -0.375 to 0.375
Outputs:
- updated: float32 [8, 4, 128, 4, 8, 128], P(None, 'prow', None, None, 'pcol')
Inputs may be any that keep to these rules, and one draw needn't show every extreme that they name: trailing is symmetric as a matrix of order 4096.
All inputs are finite; a program needn't handle non-finite values.
Results may differ from a plain program's by a relative error of at most 0.00011.
Values sent between devices are 32-bit elements; how exact they have to be, the bound alone decides.
No kernel may reach another device: no remote copies, remote signals or barrier semaphores. Data moves between devices by JAX's collectives and lax.ppermute only.
A program may use at most 64 MiB of HBM per device.

v0:
```python
import functools

import jax
import jax.numpy as jnp
from jax import lax
from jax.experimental import pallas as pl
from jax.experimental.pallas import tpu as pltpu
from jax.sharding import PartitionSpec as P

BOTH = ("prow", "pcol")
F32 = jnp.float32
BF16 = jnp.bfloat16
VMEM = pltpu.CompilerParams(vmem_limit_bytes=8 * 1024 * 1024)


def split(values):
    high = values.astype(BF16)
    return high, (values - high.astype(F32)).astype(BF16)


def dot(left, right, dims=((1,), (0,))):
    return lax.dot_general(left, right, (dims, ((), ())), preferred_element_type=F32)


def dot3(left, right, dims=((1,), (0,))):
    (lh, ll), (rh, rl) = left, right
    return dot(lh, rh, dims) + (dot(lh, rl, dims) + dot(ll, rh, dims))


def swap(values, axis, mask):
    n = lax.axis_size(axis)
    return lax.ppermute(values, axis, [(i, i ^ mask) for i in range(n)])


def halving(n):
    masks = []
    while n > 1:
        n //= 2
        masks.append(n)
    return masks


def join(values, other, high):
    pair = jnp.stack([jnp.where(high, other, values), jnp.where(high, values, other)])
    return pair.reshape((-1,) + values.shape[1:])


def gather(values, axis, masks, above):
    values = values[None]
    for mask in masks:
        values = join(values, swap(values, axis, mask), above[mask])
    return values


def slot(index, masks):
    return sum(1 << j for j, mask in enumerate(masks) if index & mask)


def swap_three(values, axis):
    return [swap(values, axis, mask) for mask in (1, 2, 3)]


def split_block_kernel(col_tiles, tile, a_ref, high_ref, low_ref):
    rows = high_ref.shape[0]
    for b in range(col_tiles):
        cols = slice(b * tile, (b + 1) * tile)
        high, low = split(a_ref[pl.ds(b, rows, stride=col_tiles), :])
        high_ref[:, cols] = high
        low_ref[:, cols] = low


def product_kernel(orders, ah_ref, al_ref, first_ref, second_ref, y_ref, keep_ref, send_ref, yh, yl, total):
    nc, half, width, tile = first_ref.shape
    for chunk, (ref, masks) in enumerate(zip((first_ref, second_ref), orders)):
        for a in range(half):
            at = chunk * half + a
            for j in range(nc):
                y_ref[at, j * width : (j + 1) * width, :] = ref[slot(j, masks), a]
            cols = slice(at * tile, (at + 1) * tile)
            yh[:, cols], yl[:, cols] = split(y_ref[at])
    total[...] = dot3((yh[...], yl[...]), (ah_ref[...], al_ref[...]))
    core = lax.axis_index("prow") & 1
    count, part = keep_ref.shape[:2]
    for y in range(count):
        keep_ref[y] = total[pl.ds(pl.multiple_of((2 * y + core) * part, part), part), :]
        send_ref[y] = total[pl.ds(pl.multiple_of((2 * y + 1 - core) * part, part), part), :]


def inner_kernel(first_ref, second_ref, y_ref, inner_ref):
    row_tiles, nb, tile = y_ref.shape
    ratio, half, cols = first_ref.shape
    inner = jnp.zeros((2 * half, nb), F32)
    for g in range(ratio):
        for b in range(cols // tile):
            at = slice(b * tile, (b + 1) * tile)
            left = jnp.concatenate([first_ref[g, :, at], second_ref[g, :, at]], axis=0)
            inner += dot3(split(left), split(y_ref[b * ratio + g]), ((1,), (1,)))
    for side in range(2):
        inner_ref[:, side * nb : (side + 1) * nb] = inner[side * half : (side + 1) * half]


def stack_left(values):
    high, low = split(values)
    return jnp.concatenate([high, high, low], axis=1)


def stack_right(ref, values):
    rows = values.shape[0]
    high, low = split(values)
    ref[:rows, :] = high
    ref[rows : 2 * rows, :] = low
    ref[2 * rows :, :] = high


def row_factor_kernel(t_ref, y_ref, out_ref):
    row_tiles, nb, tile = y_ref.shape
    factor = split(t_ref[...])
    for a in range(row_tiles):
        out_ref[a * tile : (a + 1) * tile, :] = stack_left(dot3(factor, split(y_ref[a])).T)


def column_factor_kernel(order, t_ref, cols_ref, out_ref, z_ref, y):
    slots, _, half, _ = cols_ref.shape
    for s in range(slots):
        for side in range(2):
            rows = slice((2 * s + side) * half, (2 * s + side + 1) * half)
            z_ref[rows, :] = cols_ref[slot(s, order), side]
            y[rows, :] = cols_ref[slot(s, order), 2 + side]
    stack_right(out_ref, dot3(split(t_ref[...]), split(y[...])))


def rows_kernel(orders, a_ref, uc_ref, first_ref, second_ref, came_ref, out_ref, zt):
    ratio, nb, cols = zt.shape
    half = first_ref.shape[1]
    slots = nb // (2 * half)
    rows = out_ref.shape[0]
    tile = a_ref.shape[1]
    col_tiles = cols // tile
    first_order, second_order = orders
    last = second_order[-1]
    bit = (lax.axis_index("pcol") // last) & 1
    for g in range(ratio):
        for s in range(slots):
            zt[g, 2 * s * half : (2 * s + 1) * half, :] = first_ref[slot(g * slots + s, first_order)]
            if s & last == 0:
                for ref, place in ((second_ref, bit), (came_ref, 1 - bit)):
                    at = pl.multiple_of((2 * s + 1) * half + place * (2 * last * half), half)
                    zt[g, pl.ds(at, half), :] = ref[slot(g * slots + s, second_order[:-1])]
    wide = 2
    for i in range(0, col_tiles, wide):
        turned = [zt[g, :, b * tile : (b + 1) * tile].T for b in range(i, i + wide) for g in range(ratio)]
        total = dot(stack_left(jnp.concatenate(turned, axis=0)), uc_ref[...])
        for g in range(ratio * wide):
            at = i * ratio + g
            for b in range(col_tiles):
                values = a_ref[pl.ds(at * tile * col_tiles + b, tile, stride=col_tiles), :]
                cut = slice(b * tile, (b + 1) * tile)
                out_ref[at * tile : (at + 1) * tile, cut] = values - total[g * tile : (g + 1) * tile, cut]


def update_kernel(inner_upper, rest_ref, ur_ref, uc_ref, zc_ref, *refs):
    inners, (out_ref, inner, w, result, write) = refs[:4], refs[4:]
    near = lax.axis_index("pcol") & 3
    nb, cols = zc_ref.shape
    half = inners[0].shape[1]
    slots = nb // (2 * half)
    chunks, lines, tile = result.shape
    col_tiles = cols // tile
    rows = lines // col_tiles
    writes = [pltpu.make_async_copy(result.at[i], out_ref.at[pl.ds(i * lines, lines)], write.at[i]) for i in range(chunks)]
    for r in range(4):
        for u in range(slots // 4):
            for side in range(2):
                at = pl.multiple_of((2 * (u * 4 + (near ^ r)) + side) * half, half)
                inner[pl.ds(at, half), :] = inners[r][slot(u, inner_upper), :, side * nb : (side + 1) * nb]
    stack_right(w, zc_ref[...] - dot3(split(inner[...]), (uc_ref[:nb, :], uc_ref[nb : 2 * nb, :])))
    for i in range(chunks):
        at = slice(i * rows, (i + 1) * rows)
        total = rest_ref[at, :] - dot(ur_ref[at, :], w[...])
        for g in range(rows // tile):
            for b in range(col_tiles):
                line = pl.ds(g * tile * col_tiles + b, tile, stride=col_tiles)
                result[i, line, :] = total[g * tile : (g + 1) * tile, b * tile : (b + 1) * tile]
        writes[i].start()
    for copy in writes:
        copy.wait()


def shape(*dims, dtype=F32):
    return jax.ShapeDtypeStruct(dims, dtype)


def per_device(trailing, reflectors, tfactor):
    row_tiles, _, tile, col_tiles = trailing.shape[:4]
    np_, nc = lax.axis_size("prow"), lax.axis_size("pcol")
    ratio = nc // np_
    ny = np_ // 2
    rows, cols = row_tiles * tile, col_tiles * tile
    nb = tfactor.shape[0]
    part = nb // np_
    half = row_tiles // 2
    block = trailing.reshape(rows * col_tiles, tile)
    mine = jnp.transpose(reflectors.reshape(row_tiles, tile, -1), (0, 2, 1))

    masks, cols_order = halving(nc), halving(np_)
    lead, rest = masks[: len(masks) - len(cols_order)], masks[len(masks) - len(cols_order) :]
    shift = len(cols_order)
    prow, pcol = lax.axis_index("prow").astype(jnp.int32), lax.axis_index("pcol").astype(jnp.int32)
    group = pcol >> shift
    where = {
        "group": group,
        "rounds": [(prow >> 1) ^ r for r in range(ny)],
        "share": (pcol & (np_ - 1)) * part,
        "col": {mask: (pcol & mask) != 0 for mask in masks},
        "row": {mask: (prow & mask) != 0 for mask in cols_order},
        "half": {mask: [jnp.where((prow & mask) != 0, 1 - side, side) for side in range(2)] for mask in cols_order},
    }
    mine, where = lax.optimization_barrier((mine, where))
    group, col, row = where["group"], where["col"], where["row"]
    whole = pl.BlockSpec(memory_space=pltpu.VMEM)

    def flat(p, q):
        return p * nc + q

    def turn(values, r):
        perm = [
            (flat(p, g * np_ + s), flat(s, g * np_ + (p ^ r))) for p in range(np_) for g in range(ratio) for s in range(np_)
        ]
        return lax.ppermute(values, BOTH, perm)

    inner_upper = [mask // 4 for mask in rest[:-2]]
    far, close = rest[-2:]
    orders = (masks, masks[:-2] + [close, far])
    a_high, a_low = pl.pallas_call(
        functools.partial(split_block_kernel, col_tiles, tile),
        out_shape=[shape(rows, cols, dtype=BF16)] * 2,
        in_specs=[whole],
        out_specs=[whole] * 2,
        compiler_params=VMEM,
        cost_estimate=pl.CostEstimate(flops=rows * cols * 4, bytes_accessed=rows * cols * 8, transcendentals=0),
    )(block)
    first, second = lax.optimization_barrier(mine[None, :half]), lax.optimization_barrier(mine[None, half:])
    for at, (mask, other) in enumerate(zip(*orders)):
        first_came, second_came = swap(first, "pcol", mask), swap(second, "pcol", other)
        if at == 0:
            second_came, a_high, a_low = lax.optimization_barrier((second_came, a_high, a_low))
        first, second = join(first, first_came, col[mask]), join(second, second_came, col[other])

    y_rows, keep, send = pl.pallas_call(
        functools.partial(product_kernel, orders),
        out_shape=[shape(row_tiles, nb, tile), shape(ny, part, cols), shape(ny, part, cols)],
        in_specs=[whole] * 4,
        out_specs=[whole] * 3,
        scratch_shapes=[pltpu.VMEM((nb, rows), BF16), pltpu.VMEM((nb, rows), BF16), pltpu.VMEM((nb, cols), F32)],
        compiler_params=VMEM,
        cost_estimate=pl.CostEstimate(flops=6 * nb * rows * cols, bytes_accessed=rows * cols * 8, transcendentals=0),
    )(a_high, a_low, first, second)
    other = swap(send, "prow", 1)
    kept = keep + other
    y_piece = lax.dynamic_slice(
        y_rows.reshape(col_tiles, ratio, nb, tile), (0, group, where["share"], 0), (col_tiles, 1, part, tile)
    )
    y_piece = jnp.transpose(y_piece.reshape(col_tiles, part, tile), (1, 0, 2)).reshape(part, cols)

    turned = []
    for r in range(ny):
        message = lax.dynamic_index_in_dim(kept, where["rounds"][r], 0, keepdims=False)
        turned.append(turn(message, 2 * r))
    turned = sum(turned[1:], turned[0])
    y_piece, kept = lax.optimization_barrier((y_piece, kept))
    for mask in cols_order[:-1]:
        low, high = where["half"][mask]
        pair = kept.reshape(2, mask // 2, part, cols)
        kept = lax.dynamic_index_in_dim(pair, low, 0, keepdims=False)
        kept = kept + swap(lax.dynamic_index_in_dim(pair, high, 0, keepdims=False), "prow", mask)
    piece = kept.reshape(part, cols)
    y_cols = turn(y_piece, 0).reshape(2, part // 2, cols)
    u_rows = pl.pallas_call(
        row_factor_kernel,
        out_shape=shape(rows, 3 * nb, dtype=BF16),
        in_specs=[whole] * 2,
        out_specs=whole,
        compiler_params=VMEM,
        cost_estimate=pl.CostEstimate(flops=6 * nb * nb * rows, bytes_accessed=rows * nb * 8, transcendentals=0),
    )(tfactor, y_rows)
    turned, u_rows = lax.optimization_barrier((turned, u_rows))
    first, second = turned[None, : part // 2], turned[None, part // 2 :]
    first, second = lax.optimization_barrier(first), lax.optimization_barrier(second)
    columns = jnp.concatenate([piece.reshape(2, part // 2, cols), y_cols])
    for mask in lead:
        first = join(first, swap(first, "pcol", mask), col[mask])
        second = join(second, swap(second, "pcol", mask), col[mask])
    first, columns = lax.optimization_barrier((first, columns))
    first_group, second_group = first, second
    for mask in rest[:-2]:
        first = join(first, swap(first, "pcol", mask), col[mask])
        second = join(second, swap(second, "pcol", mask), col[mask])
    first = join(first, swap(first, "pcol", far), col[far])
    second = join(second, swap(second, "pcol", close), col[close])

    columns = gather(columns, "prow", cols_order, row)
    first, y_rows = lax.optimization_barrier((first, y_rows))
    inner = pl.pallas_call(
        inner_kernel,
        out_shape=shape(part // 2, 2 * nb),
        in_specs=[whole] * 3,
        out_specs=whole,
        compiler_params=VMEM,
        cost_estimate=pl.CostEstimate(flops=6 * nb * part * cols, bytes_accessed=cols * nb * 4, transcendentals=0),
    )(first_group, second_group, y_rows)
    for mask in cols_order[::-1]:
        inner = inner + swap(inner, "prow", mask)
    inner = inner[None]
    for mask in rest[:-2]:
        inner = join(inner, swap(inner, "pcol", mask), col[mask])
    u_cols, zc = pl.pallas_call(
        functools.partial(column_factor_kernel, cols_order),
        out_shape=[shape(3 * nb, cols, dtype=BF16), shape(nb, cols)],
        in_specs=[whole] * 2,
        out_specs=[whole] * 2,
        scratch_shapes=[pltpu.VMEM((nb, cols), F32)],
        compiler_params=VMEM,
        cost_estimate=pl.CostEstimate(flops=6 * nb * nb * cols, bytes_accessed=cols * nb * 8, transcendentals=0),
    )(tfactor, columns)

    near_inner = [inner] + [swap(inner, "pcol", mask) for mask in (close, far, close + far)]
    first = join(first, swap(first, "pcol", close), col[close])
    second_came = swap(second, "pcol", far)

    remainder = pl.pallas_call(
        functools.partial(rows_kernel, orders),
        out_shape=shape(rows, cols),
        in_specs=[whole] * 5,
        out_specs=whole,
        scratch_shapes=[pltpu.VMEM((ratio, nb, cols), F32)],
        compiler_params=VMEM,
        cost_estimate=pl.CostEstimate(flops=6 * nb * rows * cols, bytes_accessed=rows * cols * 8, transcendentals=0),
    )(block, u_cols, first, second, second_came)
    chunks = 4
    lines = rows * col_tiles // chunks
    result = pl.pallas_call(
        functools.partial(update_kernel, inner_upper),
        out_shape=shape(rows * col_tiles, tile),
        in_specs=[whole] * 8,
        out_specs=pl.BlockSpec(memory_space=pltpu.HBM),
        scratch_shapes=[
            pltpu.VMEM((nb, nb), F32),
            pltpu.VMEM((3 * nb, cols), BF16),
            pltpu.VMEM((chunks, lines, tile), F32),
            pltpu.SemaphoreType.DMA((chunks,)),
        ],
        compiler_params=VMEM,
        cost_estimate=pl.CostEstimate(flops=6 * nb * rows * cols, bytes_accessed=rows * cols * 8, transcendentals=0),
    )(remainder, u_rows, u_cols, zc, *near_inner)
    return result.reshape(trailing.shape)


def solution(mesh):
    return jax.shard_map(
        per_device,
        mesh=mesh,
        in_specs=(P(None, "prow", None, None, "pcol", None), P(None, "prow", None, "pcol"), P()),
        out_specs=P(None, "prow", None, None, "pcol", None),
        check_vma=False,
    )
```

profile of v0, /device:TPU:0, one launch (start us, length us, event | category | flops | bytes accessed | tf_op | source)
XLA Modules:
  0.0 67.3 jit_solution(6804218304833847610)
XLA Ops:
  0.0 0.9 %slice_bitcast_fusion.2 = (f32[1,4,32,128]{3,2,1,0:T(8,128)S(1)}, f32[1,4,32,128]{3,2,1,0:T(8,128)S(1)}) fusion(f32[8,32,128]{2,1,0:T(8,128)} %bitcast.146), kind=kLoop, calls=%fused_computation.48 | loop fusion | bytes 262144 | tf_op jit(solution)/shard_map/broadcast_in_dim | solution.py:242
  0.9 4.1 %collective-permute-start.1 = (f32[1,4,32,128]{3,2,1,0:T(8,128)S(1)}, f32[1,4,32,128]{3,2,1,0:T(8,128)S(1)}, u32[]{:S(2)}, u32[]{:S(2)}) collective-permute-start(f32[1,4,32,128]{3,2,1,0:T(8,128)S(1)} %get-tuple-element.95), channel_id=1, source_target_pairs={{0,4},{1,5},{2,6},{3,7},{4,0},{5,1},{6,2},{7,3},{8,12},{9,13},{10,... | collective-permute-start | bytes 196616 | tf_op jit(solution)/shard_map/ppermute | solution.py:32
  5.0 0.1 collective-permute-start
  5.1 1.6 %copy-done = f32[8,1,128,4,1,128]{5,4,3,2,1,0:T(1,128)S(1)} copy-done((f32[8,1,128,4,1,128]{5,4,3,2,1,0:T(1,128)S(1)}, f32[8,1,128,4,1,128]{5,4,3,2,1,0:T(1,128)}, u32[]{:S(2)}) %copy-start) | copy-done | bytes 2097176
  6.7 0.5 shard_map.37
  7.2 1.5 %collective-permute-done.1 = f32[1,4,32,128]{3,2,1,0:T(8,128)S(1)} collective-permute-done((f32[1,4,32,128]{3,2,1,0:T(8,128)S(1)}, f32[1,4,32,128]{3,2,1,0:T(8,128)S(1)}, u32[]{:S(2)}, u32[]{:S(2)}) %collective-permute-start.1) | collective-permute-done | bytes 65568 | tf_op jit(solution)/shard_map/ppermute | solution.py:32
  8.7 2.1 %collective-permute-start.2 = (f32[2,4,32,128]{3,2,1,0:T(8,128)S(1)}, f32[2,4,32,128]{3,2,1,0:T(8,128)S(1)}, u32[]{:S(2)}, u32[]{:S(2)}) collective-permute-start(f32[2,4,32,128]{3,2,1,0:T(8,128)S(1)} %maximum_bitcast_fusion.1), channel_id=1, source_target_pairs={{0,2},{1,3},{2,0},{3,1},{4,6},{5,7},{6,4},{7,5},{8,10},{9,11},{10,... | collective-permute-start | bytes 393224 | tf_op jit(solution)/shard_map/ppermute | solution.py:32
  10.8 0.6 collective-permute-done
  11.5 1.8 %collective-permute-start.4 = (f32[2,4,32,128]{3,2,1,0:T(8,128)S(1)}, f32[2,4,32,128]{3,2,1,0:T(8,128)S(1)}, u32[]{:S(2)}, u32[]{:S(2)}) collective-permute-start(f32[2,4,32,128]{3,2,1,0:T(8,128)S(1)} %maximum_bitcast_fusion.2), channel_id=1, source_target_pairs={{0,1},{1,0},{2,3},{3,2},{4,5},{5,4},{6,7},{7,6},{8,9},{9,8},{10,11... | collective-permute-start | bytes 393224 | tf_op jit(solution)/shard_map/ppermute | solution.py:32
  13.2 1.1 %collective-permute-done.2 = f32[2,4,32,128]{3,2,1,0:T(8,128)S(1)} collective-permute-done((f32[2,4,32,128]{3,2,1,0:T(8,128)S(1)}, f32[2,4,32,128]{3,2,1,0:T(8,128)S(1)}, u32[]{:S(2)}, u32[]{:S(2)}) %collective-permute-start.2) | collective-permute-done | bytes 131104 | tf_op jit(solution)/shard_map/ppermute | solution.py:32
  14.4 1.6 %collective-permute-start.3 = (f32[4,4,32,128]{3,2,1,0:T(8,128)S(1)}, f32[4,4,32,128]{3,2,1,0:T(8,128)S(1)}, u32[]{:S(2)}, u32[]{:S(2)}) collective-permute-start(f32[4,4,32,128]{3,2,1,0:T(8,128)S(1)} %bitcast.143), channel_id=1, source_target_pairs={{0,1},{1,0},{2,3},{3,2},{4,5},{5,4},{6,7},{7,6},{8,9},{9,8},{10,11... | collective-permute-start | bytes 786440 | tf_op jit(solution)/shard_map/ppermute | solution.py:32
  16.1 0.8 %collective-permute-done.4 = f32[2,4,32,128]{3,2,1,0:T(8,128)S(1)} collective-permute-done((f32[2,4,32,128]{3,2,1,0:T(8,128)S(1)}, f32[2,4,32,128]{3,2,1,0:T(8,128)S(1)}, u32[]{:S(2)}, u32[]{:S(2)}) %collective-permute-start.4) | collective-permute-done | bytes 131104 | tf_op jit(solution)/shard_map/ppermute | solution.py:32
  17.0 0.9 %collective-permute-start.5 = (f32[4,4,32,128]{3,2,1,0:T(8,128)S(1)}, f32[4,4,32,128]{3,2,1,0:T(8,128)S(1)}, u32[]{:S(2)}, u32[]{:S(2)}) collective-permute-start(f32[4,4,32,128]{3,2,1,0:T(8,128)S(1)} %bitcast.144), channel_id=1, source_target_pairs={{0,2},{1,3},{2,0},{3,1},{4,6},{5,7},{6,4},{7,5},{8,10},{9,11},{10,... | collective-permute-start | bytes 786440 | tf_op jit(solution)/shard_map/ppermute | solution.py:32
  17.9 4.5 %collective-permute-done.3 = f32[4,4,32,128]{3,2,1,0:T(8,128)S(1)} collective-permute-done((f32[4,4,32,128]{3,2,1,0:T(8,128)S(1)}, f32[4,4,32,128]{3,2,1,0:T(8,128)S(1)}, u32[]{:S(2)}, u32[]{:S(2)}) %collective-permute-start.3) | collective-permute-done | bytes 262176 | tf_op jit(solution)/shard_map/ppermute | solution.py:32
  22.3 1.6 %collective-permute-done.5 = f32[4,4,32,128]{3,2,1,0:T(8,128)S(1)} collective-permute-done((f32[4,4,32,128]{3,2,1,0:T(8,128)S(1)}, f32[4,4,32,128]{3,2,1,0:T(8,128)S(1)}, u32[]{:S(2)}, u32[]{:S(2)}) %collective-permute-start.5) | collective-permute-done | bytes 262176 | tf_op jit(solution)/shard_map/ppermute | solution.py:32
  23.9 0.1 select_bitcast_fusion.7
  24.2 0.0 copy-start.2
  24.2 1.1 %shard_map.38 = (f32[8,256,128]{2,1,0:T(8,128)S(1)}, f32[2,64,512]{2,1,0:T(8,128)S(1)}, f32[2,64,512]{2,1,0:T(8,128)S(1)}) custom-call(bf16[1024,512]{1,0:T(8,128)(2,1)S(1)} %get-tuple-element.41.ah_ref, bf16[1024,512]{1,0:T(8,128)(2,1)S(1)} %get-tuple-element.42.al_ref, f32[8,4,32,128]{3,2,1,0:T(8,128)S(1)} %bitcast.137, f32[8,4,32,128]{3,2,1,0:T(8,128)S(1)} %bitcast.136), custom_call_target="tpu_custom_call" | custom-call | flops 805306368 | bytes 4194304 | tf_op jit(solution)/shard_map/pallas_call | solution.py:249
  25.2 0.1 collective-permute-start.6
  25.4 1.5 %collective-permute-done.6 = f32[2,64,512]{2,1,0:T(8,128)S(1)} collective-permute-done((f32[2,64,512]{2,1,0:T(8,128)S(1)}, f32[2,64,512]{2,1,0:T(8,128)S(1)}, u32[]{:S(2)}, u32[]{:S(2)}) %collective-permute-start.6) | collective-permute-done | bytes 262176 | tf_op jit(solution)/shard_map/ppermute | solution.py:32
  26.9 1.1 %collective-permute-start.8 = (f32[64,512]{1,0:T(8,128)S(1)}, f32[64,512]{1,0:T(8,128)S(1)}, u32[]{:S(2)}, u32[]{:S(2)}) collective-permute-start(f32[64,512]{1,0:T(8,128)S(1)} %get-tuple-element.79), channel_id=1, source_target_pairs={{0,2},{1,10},{2,18},{3,26},{4,6},{5,14},{6,22},{7,30},{8,3},{9,11}... | collective-permute-start | bytes 393224 | tf_op jit(solution)/shard_map/ppermute | solution.py:229
  28.1 0.7 collective-permute-start.7
  28.7 0.0 copy-done.2
  28.7 1.0 %shard_map.39.ur_ref = bf16[1024,768]{1,0:T(8,128)(2,1)S(1)} custom-call(f32[256,256]{1,0:T(8,128)S(1)} %copy-done.2, f32[8,256,128]{2,1,0:T(8,128)S(1)} %get-tuple-element.64.y_ref), custom_call_target="tpu_custom_call" | custom-call | flops 402653184 | bytes 2097152 | tf_op jit(solution)/shard_map/pallas_call | solution.py:278
  29.8 4.3 %collective-permute-start.10 = (f32[1,64,512]{2,1,0:T(8,128)S(1)}, f32[1,64,512]{2,1,0:T(8,128)S(1)}, u32[]{:S(2)}, u32[]{:S(2)}) collective-permute-start(f32[1,64,512]{2,1,0:T(8,128)S(1)} %constant_dynamic-slice_fusion), channel_id=1, source_target_pairs={{0,16},{8,24},{16,0},{24,8},{1,17},{9,25},{17,1},{25,9},{2,18},{10... | collective-permute-start | bytes 393224 | tf_op jit(solution)/shard_map/ppermute | solution.py:32
  34.1 0.7 collective-permute-start.11
  34.8 0.0 collective-permute-done.8
  34.8 0.0 collective-permute-done.7
  34.8 3.4 %collective-permute-start.9 = (f32[1,32,512]{2,1,0:T(8,128)S(1)}, f32[1,32,512]{2,1,0:T(8,128)S(1)}, u32[]{:S(2)}, u32[]{:S(2)}) collective-permute-start(f32[1,32,512]{2,1,0:T(8,128)S(1)} %get-tuple-element.88), channel_id=1, source_target_pairs={{0,4},{1,5},{2,6},{3,7},{4,0},{5,1},{6,2},{7,3},{8,12},{9,13},{10,... | collective-permute-start | bytes 196616 | tf_op jit(solution)/shard_map/ppermute | solution.py:32
  38.3 0.1 collective-permute-start.16
  38.4 3.7 %collective-permute-done.10 = f32[1,64,512]{2,1,0:T(8,128)S(1)} collective-permute-done((f32[1,64,512]{2,1,0:T(8,128)S(1)}, f32[1,64,512]{2,1,0:T(8,128)S(1)}, u32[]{:S(2)}, u32[]{:S(2)}) %collective-permute-start.10) | collective-permute-done | bytes 131104 | tf_op jit(solution)/shard_map/ppermute | solution.py:32
  42.1 0.0 collective-permute-done.11
  42.1 0.0 collective-permute-done.9
  42.2 4.1 %collective-permute-start.14 = (f32[2,32,512]{2,1,0:T(8,128)S(1)}, f32[2,32,512]{2,1,0:T(8,128)S(1)}, u32[]{:S(2)}, u32[]{:S(2)}) collective-permute-start(f32[2,32,512]{2,1,0:T(8,128)S(1)} %maximum_bitcast_fusion.3.first_ref), channel_id=1, source_target_pairs={{0,2},{1,3},{2,0},{3,1},{4,6},{5,7},{6,4},{7,5},{8,10},{9,11},{10,... | collective-permute-start | bytes 393224 | tf_op jit(solution)/shard_map/ppermute | solution.py:32
  46.3 0.0 collective-permute-done.16
  46.3 1.4 %collective-permute-start.17 = (f32[2,32,512]{2,1,0:T(8,128)S(1)}, f32[2,32,512]{2,1,0:T(8,128)S(1)}, u32[]{:S(2)}, u32[]{:S(2)}) collective-permute-start(f32[2,32,512]{2,1,0:T(8,128)S(1)} %maximum_bitcast_fusion.4.second_ref), channel_id=1, source_target_pairs={{0,1},{1,0},{2,3},{3,2},{4,5},{5,4},{6,7},{7,6},{8,9},{9,8},{10,11... | collective-permute-start | bytes 393224 | tf_op jit(solution)/shard_map/ppermute | solution.py:32
  47.7 0.4 collective-permute-start.12
  48.2 2.5 %collective-permute-done.14 = f32[2,32,512]{2,1,0:T(8,128)S(1)} collective-permute-done((f32[2,32,512]{2,1,0:T(8,128)S(1)}, f32[2,32,512]{2,1,0:T(8,128)S(1)}, u32[]{:S(2)}, u32[]{:S(2)}) %collective-permute-start.14) | collective-permute-done | bytes 131104 | tf_op jit(solution)/shard_map/ppermute | solution.py:32
  50.7 0.7 shard_map.42
  51.3 0.1 collective-permute-start.19
  51.4 0.1 collective-permute-start.15
  51.5 0.8 %collective-permute-done.17 = f32[2,32,512]{2,1,0:T(8,128)S(1)} collective-permute-done((f32[2,32,512]{2,1,0:T(8,128)S(1)}, f32[2,32,512]{2,1,0:T(8,128)S(1)}, u32[]{:S(2)}, u32[]{:S(2)}) %collective-permute-start.17) | collective-permute-done | bytes 131104 | tf_op jit(solution)/shard_map/ppermute | solution.py:32
  52.4 1.1 %collective-permute-start.18 = (f32[4,32,512]{2,1,0:T(8,128)S(1)}, f32[4,32,512]{2,1,0:T(8,128)S(1)}, u32[]{:S(2)}, u32[]{:S(2)}) collective-permute-start(f32[4,32,512]{2,1,0:T(8,128)S(1)} %bitcast.138), channel_id=1, source_target_pairs={{0,2},{1,3},{2,0},{3,1},{4,6},{5,7},{6,4},{7,5},{8,10},{9,11},{10,... | collective-permute-start | bytes 786440 | tf_op jit(solution)/shard_map/ppermute | solution.py:32
  53.5 0.0 collective-permute-done.19
  53.5 0.8 %collective-permute-start.20 = (f32[32,512]{1,0:T(8,128)S(1)}, f32[32,512]{1,0:T(8,128)S(1)}, u32[]{:S(2)}, u32[]{:S(2)}) collective-permute-start(f32[32,512]{1,0:T(8,128)S(1)} %add.44), channel_id=1, source_target_pairs={{0,16},{8,24},{16,0},{24,8},{1,17},{9,25},{17,1},{25,9},{2,18},{10... | collective-permute-start | bytes 196616 | tf_op jit(solution)/shard_map/ppermute | solution.py:32
  54.3 1.9 %collective-permute-done.12 = f32[1,4,32,512]{3,2,1,0:T(8,128)S(1)} collective-permute-done((f32[1,4,32,512]{3,2,1,0:T(8,128)S(1)}, f32[1,4,32,512]{3,2,1,0:T(8,128)S(1)}, u32[]{:S(2)}, u32[]{:S(2)}) %collective-permute-start.12) | collective-permute-done | bytes 262176 | tf_op jit(solution)/shard_map/ppermute | solution.py:32
  56.3 0.1 collective-permute-start.13
  56.4 1.4 %collective-permute-done.20 = f32[32,512]{1,0:T(8,128)S(1)} collective-permute-done((f32[32,512]{1,0:T(8,128)S(1)}, f32[32,512]{1,0:T(8,128)S(1)}, u32[]{:S(2)}, u32[]{:S(2)}) %collective-permute-start.20) | collective-permute-done | bytes 65568 | tf_op jit(solution)/shard_map/ppermute | solution.py:32
  57.9 1.7 %collective-permute-start.23 = (f32[1,32,512]{2,1,0:T(8,128)S(1)}, f32[1,32,512]{2,1,0:T(8,128)S(1)}, u32[]{:S(2)}, u32[]{:S(2)}) collective-permute-start(f32[1,32,512]{2,1,0:T(8,128)S(1)} %add_bitcast_fusion.refs_0_), channel_id=1, source_target_pairs={{0,3},{1,2},{2,1},{3,0},{4,7},{5,6},{6,5},{7,4},{8,11},{9,10},{10,... | collective-permute-start | bytes 196616 | tf_op jit(solution)/shard_map/ppermute | solution.py:32
  59.6 1.3 %collective-permute-start.22 = (f32[1,32,512]{2,1,0:T(8,128)S(1)}, f32[1,32,512]{2,1,0:T(8,128)S(1)}, u32[]{:S(2)}, u32[]{:S(2)}) collective-permute-start(f32[1,32,512]{2,1,0:T(8,128)S(1)} %add_bitcast_fusion.refs_0_), channel_id=1, source_target_pairs={{0,2},{1,3},{2,0},{3,1},{4,6},{5,7},{6,4},{7,5},{8,10},{9,11},{10,... | collective-permute-start | bytes 196616 | tf_op jit(solution)/shard_map/ppermute | solution.py:32
  60.9 0.0 collective-permute-done.15
  60.9 0.6 collective-permute-start.21
  61.5 0.0 collective-permute-done.13
  61.5 0.1 select_bitcast_fusion.1
  61.7 0.0 copy-start.1
  61.7 0.1 pad_maximum_fusion
  61.8 0.4 shard_map.40
  62.2 0.0 collective-permute-done.18.came_ref
  62.2 1.0 %copy-done.1 = f32[8,1,128,4,1,128]{5,4,3,2,1,0:T(1,128)S(1)} copy-done((f32[8,1,128,4,1,128]{5,4,3,2,1,0:T(1,128)S(1)}, f32[8,1,128,4,1,128]{5,4,3,2,1,0:T(1,128)}, u32[]{:S(2)}) %copy-start.1) | copy-done | bytes 2097176
  63.3 1.1 %shard_map.41.rest_ref = f32[1024,512]{1,0:T(8,128)S(1)} custom-call(f32[4096,128]{1,0:T(8,128)S(1)} %bitcast.132, bf16[768,512]{1,0:T(8,128)(2,1)S(1)} %get-tuple-element.59.uc_ref, f32[8,32,512]{2,1,0:T(8,128)S(1)} %bitcast.135, f32[4,32,512]{2,1,0:T(8,128)S(1)} %bitcast.139, f32[4,32,512]{2,1,0:T(8,128)S(1)} %collective-permute-done.18.came_ref), custom_call_target="tpu_custom_call" | custom-call | flops 805306368 | bytes 4194304 | tf_op jit(solution)/shard_map/pallas_call | solution.py:330
  64.4 0.0 collective-permute-done.23.refs_3_
  64.4 0.0 collective-permute-done.22.refs_2_
  64.4 0.7 %collective-permute-done.21.refs_1_ = f32[1,32,512]{2,1,0:T(8,128)S(1)} collective-permute-done((f32[1,32,512]{2,1,0:T(8,128)S(1)}, f32[1,32,512]{2,1,0:T(8,128)S(1)}, u32[]{:S(2)}, u32[]{:S(2)}) %collective-permute-start.21) | collective-permute-done | bytes 65568 | tf_op jit(solution)/shard_map/ppermute | solution.py:32
  65.1 2.2 %shard_map.43 = f32[4096,128]{1,0:T(8,128)} custom-call(f32[1024,512]{1,0:T(8,128)S(1)} %shard_map.41.rest_ref, bf16[1024,768]{1,0:T(8,128)(2,1)S(1)} %shard_map.39.ur_ref, bf16[768,512]{1,0:T(8,128)(2,1)S(1)} %get-tuple-element.59.uc_ref, f32[256,512]{1,0:T(8,128)S(1)} %get-tuple-element.63.zc_ref, f32[1,32,512]{2,1,0:T(8,128)S(1)} %add_bitcast_fusion.refs_0_, ...), custom_call_target="tpu_custom_call" | custom-call | flops 805306368 | bytes 4194304 | tf_op jit(solution)/shard_map/pallas_call | solution.py:341
  (33 shorter events, 0.7 us)
Async XLA Ops:
  0.9 7.8 %collective-permute-start.1 = (f32[1,4,32,128]{3,2,1,0:T(8,128)S(1)}, f32[1,4,32,128]{3,2,1,0:T(8,128)S(1)}, u32[]{:S(2)}, u32[]{:S(2)}) collective-permute-start(f32[1,4,32,128]{3,2,1,0:T(8,128)S(1)} %get-tuple-element.95), channel_id=1, source_target_pairs={{0,4},{1,5},{2,6},{3,7},{4,0},{5,1},{6,2},{7,3},{8,12},{9,13},{10,... | collective-permute-start | bytes 196616 | tf_op jit(solution)/shard_map/ppermute | solution.py:32
  5.0 6.5 %collective-permute-start = (f32[1,4,32,128]{3,2,1,0:T(8,128)S(1)}, f32[1,4,32,128]{3,2,1,0:T(8,128)S(1)}, u32[]{:S(2)}, u32[]{:S(2)}) collective-permute-start(f32[1,4,32,128]{3,2,1,0:T(8,128)S(1)} %get-tuple-element.96), channel_id=1, source_target_pairs={{0,4},{1,5},{2,6},{3,7},{4,0},{5,1},{6,2},{7,3},{8,12},{9,13},{10,... | collective-permute-start | bytes 196616 | tf_op jit(solution)/shard_map/ppermute | solution.py:32
  5.1 1.6 %copy-start = (f32[8,1,128,4,1,128]{5,4,3,2,1,0:T(1,128)S(1)}, f32[8,1,128,4,1,128]{5,4,3,2,1,0:T(1,128)}, u32[]{:S(2)}) copy-start(f32[8,1,128,4,1,128]{5,4,3,2,1,0:T(1,128)} %param.3) | copy-start | bytes 6291460
  8.7 5.7 %collective-permute-start.2 = (f32[2,4,32,128]{3,2,1,0:T(8,128)S(1)}, f32[2,4,32,128]{3,2,1,0:T(8,128)S(1)}, u32[]{:S(2)}, u32[]{:S(2)}) collective-permute-start(f32[2,4,32,128]{3,2,1,0:T(8,128)S(1)} %maximum_bitcast_fusion.1), channel_id=1, source_target_pairs={{0,2},{1,3},{2,0},{3,1},{4,6},{5,7},{6,4},{7,5},{8,10},{9,11},{10,... | collective-permute-start | bytes 393224 | tf_op jit(solution)/shard_map/ppermute | solution.py:32
  11.5 5.4 %collective-permute-start.4 = (f32[2,4,32,128]{3,2,1,0:T(8,128)S(1)}, f32[2,4,32,128]{3,2,1,0:T(8,128)S(1)}, u32[]{:S(2)}, u32[]{:S(2)}) collective-permute-start(f32[2,4,32,128]{3,2,1,0:T(8,128)S(1)} %maximum_bitcast_fusion.2), channel_id=1, source_target_pairs={{0,1},{1,0},{2,3},{3,2},{4,5},{5,4},{6,7},{7,6},{8,9},{9,8},{10,11... | collective-permute-start | bytes 393224 | tf_op jit(solution)/shard_map/ppermute | solution.py:32
  14.4 7.9 %collective-permute-start.3 = (f32[4,4,32,128]{3,2,1,0:T(8,128)S(1)}, f32[4,4,32,128]{3,2,1,0:T(8,128)S(1)}, u32[]{:S(2)}, u32[]{:S(2)}) collective-permute-start(f32[4,4,32,128]{3,2,1,0:T(8,128)S(1)} %bitcast.143), channel_id=1, source_target_pairs={{0,1},{1,0},{2,3},{3,2},{4,5},{5,4},{6,7},{7,6},{8,9},{9,8},{10,11... | collective-permute-start | bytes 786440 | tf_op jit(solution)/shard_map/ppermute | solution.py:32
  17.0 7.0 %collective-permute-start.5 = (f32[4,4,32,128]{3,2,1,0:T(8,128)S(1)}, f32[4,4,32,128]{3,2,1,0:T(8,128)S(1)}, u32[]{:S(2)}, u32[]{:S(2)}) collective-permute-start(f32[4,4,32,128]{3,2,1,0:T(8,128)S(1)} %bitcast.144), channel_id=1, source_target_pairs={{0,2},{1,3},{2,0},{3,1},{4,6},{5,7},{6,4},{7,5},{8,10},{9,11},{10,... | collective-permute-start | bytes 786440 | tf_op jit(solution)/shard_map/ppermute | solution.py:32
  24.2 4.6 %copy-start.2 = (f32[256,256]{1,0:T(8,128)S(1)}, f32[256,256]{1,0:T(8,128)}, u32[]{:S(2)}) copy-start(f32[256,256]{1,0:T(8,128)} %t_ref.3) | copy-start | bytes 786436
  25.2 1.6 %collective-permute-start.6 = (f32[2,64,512]{2,1,0:T(8,128)S(1)}, f32[2,64,512]{2,1,0:T(8,128)S(1)}, u32[]{:S(2)}, u32[]{:S(2)}) collective-permute-start(f32[2,64,512]{2,1,0:T(8,128)S(1)} %get-tuple-element.47), channel_id=1, source_target_pairs={{0,8},{8,0},{16,24},{24,16},{1,9},{9,1},{17,25},{25,17},{2,10},{10... | collective-permute-start | bytes 786440 | tf_op jit(solution)/shard_map/ppermute | solution.py:32
  26.9 7.8 %collective-permute-start.8 = (f32[64,512]{1,0:T(8,128)S(1)}, f32[64,512]{1,0:T(8,128)S(1)}, u32[]{:S(2)}, u32[]{:S(2)}) collective-permute-start(f32[64,512]{1,0:T(8,128)S(1)} %get-tuple-element.79), channel_id=1, source_target_pairs={{0,2},{1,10},{2,18},{3,26},{4,6},{5,14},{6,22},{7,30},{8,3},{9,11}... | collective-permute-start | bytes 393224 | tf_op jit(solution)/shard_map/ppermute | solution.py:229
  28.1 6.7 %collective-permute-start.7 = (f32[64,512]{1,0:T(8,128)S(1)}, f32[64,512]{1,0:T(8,128)S(1)}, u32[]{:S(2)}, u32[]{:S(2)}) collective-permute-start(f32[64,512]{1,0:T(8,128)S(1)} %get-tuple-element.80), channel_id=1, source_target_pairs={{0,0},{1,8},{2,16},{3,24},{4,4},{5,12},{6,20},{7,28},{8,1},{9,9},{... | collective-permute-start | bytes 393224 | tf_op jit(solution)/shard_map/ppermute | solution.py:229
  29.8 12.2 %collective-permute-start.10 = (f32[1,64,512]{2,1,0:T(8,128)S(1)}, f32[1,64,512]{2,1,0:T(8,128)S(1)}, u32[]{:S(2)}, u32[]{:S(2)}) collective-permute-start(f32[1,64,512]{2,1,0:T(8,128)S(1)} %constant_dynamic-slice_fusion), channel_id=1, source_target_pairs={{0,16},{8,24},{16,0},{24,8},{1,17},{9,25},{17,1},{25,9},{2,18},{10... | collective-permute-start | bytes 393224 | tf_op jit(solution)/shard_map/ppermute | solution.py:32
  34.1 8.0 %collective-permute-start.11 = (f32[64,512]{1,0:T(8,128)S(1)}, f32[64,512]{1,0:T(8,128)S(1)}, u32[]{:S(2)}, u32[]{:S(2)}) collective-permute-start(f32[64,512]{1,0:T(8,128)S(1)} %copy_bitcast_fusion), channel_id=1, source_target_pairs={{0,0},{1,8},{2,16},{3,24},{4,4},{5,12},{6,20},{7,28},{8,1},{9,9},{... | collective-permute-start | bytes 393224 | tf_op jit(solution)/shard_map/ppermute | solution.py:229
  34.8 7.3 %collective-permute-start.9 = (f32[1,32,512]{2,1,0:T(8,128)S(1)}, f32[1,32,512]{2,1,0:T(8,128)S(1)}, u32[]{:S(2)}, u32[]{:S(2)}) collective-permute-start(f32[1,32,512]{2,1,0:T(8,128)S(1)} %get-tuple-element.88), channel_id=1, source_target_pairs={{0,4},{1,5},{2,6},{3,7},{4,0},{5,1},{6,2},{7,3},{8,12},{9,13},{10,... | collective-permute-start | bytes 196616 | tf_op jit(solution)/shard_map/ppermute | solution.py:32
  38.3 8.0 %collective-permute-start.16 = (f32[1,32,512]{2,1,0:T(8,128)S(1)}, f32[1,32,512]{2,1,0:T(8,128)S(1)}, u32[]{:S(2)}, u32[]{:S(2)}) collective-permute-start(f32[1,32,512]{2,1,0:T(8,128)S(1)} %get-tuple-element.87), channel_id=1, source_target_pairs={{0,4},{1,5},{2,6},{3,7},{4,0},{5,1},{6,2},{7,3},{8,12},{9,13},{10,... | collective-permute-start | bytes 196616 | tf_op jit(solution)/shard_map/ppermute | solution.py:32
  42.2 8.4 %collective-permute-start.14 = (f32[2,32,512]{2,1,0:T(8,128)S(1)}, f32[2,32,512]{2,1,0:T(8,128)S(1)}, u32[]{:S(2)}, u32[]{:S(2)}) collective-permute-start(f32[2,32,512]{2,1,0:T(8,128)S(1)} %maximum_bitcast_fusion.3.first_ref), channel_id=1, source_target_pairs={{0,2},{1,3},{2,0},{3,1},{4,6},{5,7},{6,4},{7,5},{8,10},{9,11},{10,... | collective-permute-start | bytes 393224 | tf_op jit(solution)/shard_map/ppermute | solution.py:32
  46.3 6.0 %collective-permute-start.17 = (f32[2,32,512]{2,1,0:T(8,128)S(1)}, f32[2,32,512]{2,1,0:T(8,128)S(1)}, u32[]{:S(2)}, u32[]{:S(2)}) collective-permute-start(f32[2,32,512]{2,1,0:T(8,128)S(1)} %maximum_bitcast_fusion.4.second_ref), channel_id=1, source_target_pairs={{0,1},{1,0},{2,3},{3,2},{4,5},{5,4},{6,7},{7,6},{8,9},{9,8},{10,11... | collective-permute-start | bytes 393224 | tf_op jit(solution)/shard_map/ppermute | solution.py:32
  47.7 8.5 %collective-permute-start.12 = (f32[1,4,32,512]{3,2,1,0:T(8,128)S(1)}, f32[1,4,32,512]{3,2,1,0:T(8,128)S(1)}, u32[]{:S(2)}, u32[]{:S(2)}) collective-permute-start(f32[1,4,32,512]{3,2,1,0:T(8,128)S(1)} %bitcast.140), channel_id=1, source_target_pairs={{0,16},{8,24},{16,0},{24,8},{1,17},{9,25},{17,1},{25,9},{2,18},{10... | collective-permute-start | bytes 786440 | tf_op jit(solution)/shard_map/ppermute | solution.py:32
  51.3 2.2 %collective-permute-start.19 = (f32[32,512]{1,0:T(8,128)S(1)}, f32[32,512]{1,0:T(8,128)S(1)}, u32[]{:S(2)}, u32[]{:S(2)}) collective-permute-start(f32[32,512]{1,0:T(8,128)S(1)} %shard_map.42), channel_id=1, source_target_pairs={{0,8},{8,0},{16,24},{24,16},{1,9},{9,1},{17,25},{25,17},{2,10},{10... | collective-permute-start | bytes 196616 | tf_op jit(solution)/shard_map/ppermute | solution.py:32
  51.4 9.5 %collective-permute-start.15 = (f32[4,32,512]{2,1,0:T(8,128)S(1)}, f32[4,32,512]{2,1,0:T(8,128)S(1)}, u32[]{:S(2)}, u32[]{:S(2)}) collective-permute-start(f32[4,32,512]{2,1,0:T(8,128)S(1)} %bitcast.141), channel_id=1, source_target_pairs={{0,1},{1,0},{2,3},{3,2},{4,5},{5,4},{6,7},{7,6},{8,9},{9,8},{10,11... | collective-permute-start | bytes 786440 | tf_op jit(solution)/shard_map/ppermute | solution.py:32
  52.4 9.8 %collective-permute-start.18 = (f32[4,32,512]{2,1,0:T(8,128)S(1)}, f32[4,32,512]{2,1,0:T(8,128)S(1)}, u32[]{:S(2)}, u32[]{:S(2)}) collective-permute-start(f32[4,32,512]{2,1,0:T(8,128)S(1)} %bitcast.138), channel_id=1, source_target_pairs={{0,2},{1,3},{2,0},{3,1},{4,6},{5,7},{6,4},{7,5},{8,10},{9,11},{10,... | collective-permute-start | bytes 786440 | tf_op jit(solution)/shard_map/ppermute | solution.py:32
  53.5 4.3 %collective-permute-start.20 = (f32[32,512]{1,0:T(8,128)S(1)}, f32[32,512]{1,0:T(8,128)S(1)}, u32[]{:S(2)}, u32[]{:S(2)}) collective-permute-start(f32[32,512]{1,0:T(8,128)S(1)} %add.44), channel_id=1, source_target_pairs={{0,16},{8,24},{16,0},{24,8},{1,17},{9,25},{17,1},{25,9},{2,18},{10... | collective-permute-start | bytes 196616 | tf_op jit(solution)/shard_map/ppermute | solution.py:32
  56.3 5.2 %collective-permute-start.13 = (f32[2,4,32,512]{3,2,1,0:T(8,128)S(1)}, f32[2,4,32,512]{3,2,1,0:T(8,128)S(1)}, u32[]{:S(2)}, u32[]{:S(2)}) collective-permute-start(f32[2,4,32,512]{3,2,1,0:T(8,128)S(1)} %maximum_bitcast_fusion), channel_id=1, source_target_pairs={{0,8},{8,0},{16,24},{24,16},{1,9},{9,1},{17,25},{25,17},{2,10},{10... | collective-permute-start | bytes 1572872 | tf_op jit(solution)/shard_map/ppermute | solution.py:32
  57.9 6.5 %collective-permute-start.23 = (f32[1,32,512]{2,1,0:T(8,128)S(1)}, f32[1,32,512]{2,1,0:T(8,128)S(1)}, u32[]{:S(2)}, u32[]{:S(2)}) collective-permute-start(f32[1,32,512]{2,1,0:T(8,128)S(1)} %add_bitcast_fusion.refs_0_), channel_id=1, source_target_pairs={{0,3},{1,2},{2,1},{3,0},{4,7},{5,6},{6,5},{7,4},{8,11},{9,10},{10,... | collective-permute-start | bytes 196616 | tf_op jit(solution)/shard_map/ppermute | solution.py:32
  59.6 4.8 %collective-permute-start.22 = (f32[1,32,512]{2,1,0:T(8,128)S(1)}, f32[1,32,512]{2,1,0:T(8,128)S(1)}, u32[]{:S(2)}, u32[]{:S(2)}) collective-permute-start(f32[1,32,512]{2,1,0:T(8,128)S(1)} %add_bitcast_fusion.refs_0_), channel_id=1, source_target_pairs={{0,2},{1,3},{2,0},{3,1},{4,6},{5,7},{6,4},{7,5},{8,10},{9,11},{10,... | collective-permute-start | bytes 196616 | tf_op jit(solution)/shard_map/ppermute | solution.py:32
  60.9 4.3 %collective-permute-start.21 = (f32[1,32,512]{2,1,0:T(8,128)S(1)}, f32[1,32,512]{2,1,0:T(8,128)S(1)}, u32[]{:S(2)}, u32[]{:S(2)}) collective-permute-start(f32[1,32,512]{2,1,0:T(8,128)S(1)} %add_bitcast_fusion.refs_0_), channel_id=1, source_target_pairs={{0,1},{1,0},{2,3},{3,2},{4,5},{5,4},{6,7},{7,6},{8,9},{9,8},{10,11... | collective-permute-start | bytes 196616 | tf_op jit(solution)/shard_map/ppermute | solution.py:32
  61.7 1.6 %copy-start.1 = (f32[8,1,128,4,1,128]{5,4,3,2,1,0:T(1,128)S(1)}, f32[8,1,128,4,1,128]{5,4,3,2,1,0:T(1,128)}, u32[]{:S(2)}) copy-start(f32[8,1,128,4,1,128]{5,4,3,2,1,0:T(1,128)} %param.3) | copy-start | bytes 6291460
where the time goes:
time: 67.5 us; the launch traced here: 67.3 us
  starting transfers between devices  32.6 us (48%)
  waiting for transfers between devices  22.8 us (34%)
  Pallas kernels  6.96 us (10%)
  local copies, waits for them, and re-layouts  3.6 us (5%)
  other arithmetic  0.96 us (1%)
    ppermute x21, starting transfers between devices, swap(): return lax.ppermute(values, axis, [(i, i ^ mask) for i in range(n)])  30.1 us
    ppermute x21, waiting for transfers between devices, swap(): return lax.ppermute(values, axis, [(i, i ^ mask) for i in range(n)])  22.8 us
    unnamed x6, local copies, waits for them, and re-layouts  2.64 us
    ppermute x3, starting transfers between devices, turn(): return lax.ppermute(values, BOTH, perm)  2.46 us
    pallas_call x1, Pallas kernels, per_device(): pl.pallas_call(functools.partial(update_kernel, inner_upper), out_shape=s...  2.15 us
  transfers between devices with their start and end apart: 24, of which 13 were waited for; matrix products, arithmetic and copies ran while one was open for 1% of the time, Pallas kernels for 6%

commit v1 on v0

--- a/solution.py
+++ b/solution.py
@@ -60,11 +60,13 @@
     return [swap(values, axis, mask) for mask in (1, 2, 3)]
 
 
-def split_block_kernel(col_tiles, tile, a_ref, high_ref, low_ref):
+def split_block_kernel(col_tiles, tile, a_ref, high_ref, low_ref, copy_ref):
     rows = high_ref.shape[0]
     for b in range(col_tiles):
         cols = slice(b * tile, (b + 1) * tile)
-        high, low = split(a_ref[pl.ds(b, rows, stride=col_tiles), :])
+        values = a_ref[pl.ds(b, rows, stride=col_tiles), :]
+        copy_ref[:, cols] = values
+        high, low = split(values)
         high_ref[:, cols] = high
         low_ref[:, cols] = low
 
@@ -129,13 +131,11 @@
     stack_right(out_ref, dot3(split(t_ref[...]), split(y[...])))
 
 
-def rows_kernel(orders, a_ref, uc_ref, first_ref, second_ref, came_ref, out_ref, zt):
+def rows_kernel(orders, col_tiles, a_ref, uc_ref, first_ref, second_ref, came_ref, out_ref, zt):
     ratio, nb, cols = zt.shape
     half = first_ref.shape[1]
     slots = nb // (2 * half)
-    rows = out_ref.shape[0]
-    tile = a_ref.shape[1]
-    col_tiles = cols // tile
+    tile = cols // col_tiles
     first_order, second_order = orders
     last = second_order[-1]
     bit = (lax.axis_index("pcol") // last) & 1
@@ -152,10 +152,8 @@
         total = dot(stack_left(jnp.concatenate(turned, axis=0)), uc_ref[...])
         for g in range(ratio * wide):
             at = i * ratio + g
-            for b in range(col_tiles):
-                values = a_ref[pl.ds(at * tile * col_tiles + b, tile, stride=col_tiles), :]
-                cut = slice(b * tile, (b + 1) * tile)
-                out_ref[at * tile : (at + 1) * tile, cut] = values - total[g * tile : (g + 1) * tile, cut]
+            cut = slice(at * tile, (at + 1) * tile)
+            out_ref[cut, :] = a_ref[cut, :] - total[g * tile : (g + 1) * tile, :]
 
 
 def update_kernel(inner_upper, rest_ref, ur_ref, uc_ref, zc_ref, *refs):
@@ -231,11 +229,11 @@
     inner_upper = [mask // 4 for mask in rest[:-2]]
     far, close = rest[-2:]
     orders = (masks, masks[:-2] + [close, far])
-    a_high, a_low = pl.pallas_call(
+    a_high, a_low, a_full = pl.pallas_call(
         functools.partial(split_block_kernel, col_tiles, tile),
-        out_shape=[shape(rows, cols, dtype=BF16)] * 2,
+        out_shape=[shape(rows, cols, dtype=BF16)] * 2 + [shape(rows, cols)],
         in_specs=[whole],
-        out_specs=[whole] * 2,
+        out_specs=[whole] * 3,
         compiler_params=VMEM,
         cost_estimate=pl.CostEstimate(flops=rows * cols * 4, bytes_accessed=rows * cols * 8, transcendentals=0),
     )(block)
@@ -328,14 +326,14 @@
     second_came = swap(second, "pcol", far)
 
     remainder = pl.pallas_call(
-        functools.partial(rows_kernel, orders),
+        functools.partial(rows_kernel, orders, col_tiles),
         out_shape=shape(rows, cols),
         in_specs=[whole] * 5,
         out_specs=whole,
         scratch_shapes=[pltpu.VMEM((ratio, nb, cols), F32)],
         compiler_params=VMEM,
         cost_estimate=pl.CostEstimate(flops=6 * nb * rows * cols, bytes_accessed=rows * cols * 8, transcendentals=0),
-    )(block, u_cols, first, second, second_came)
+    )(a_full, u_cols, first, second, second_came)
     chunks = 4
     lines = rows * col_tiles // chunks
     result = pl.pallas_call(

time: 67.5 us -> 70.3 us (1.041)
  other arithmetic: 0.96 us -> 1.99 us
  Pallas kernels: 6.96 us -> 7.96 us
  waiting for transfers between devices: 22.8 us -> 23.8 us
    ppermute x21, waiting for transfers between devices: 22.8 us -> 23.8 us  [swap(): return lax.ppermute(values, axis, [(i, i ^ mask) for i in range(n)])]
    add x1, other arithmetic: 0.04 us -> 1.06 us  [per_device(): kept = keep + other]
    pallas_call x1, Pallas kernels: 1.07 us -> 1.77 us  [per_device(): pl.pallas_call(functools.partial(product_kernel, orders), out_shape=[shap...]
  transfers between devices with their start and end apart: 24 -> 24, of which waited for: 13 -> 15; matrix products, arithmetic and copies ran while one was open for 1% -> 1% of each run, Pallas kernels for 6% -> 6%
where the time goes in v1:
time: 70.3 us; the launch traced here: 70 us
  starting transfers between devices  32.6 us (46%)
  waiting for transfers between devices  23.8 us (34%)
  Pallas kernels  7.96 us (11%)
  local copies, waits for them, and re-layouts  3.24 us (5%)
  other arithmetic  1.99 us (3%)
    ppermute x21, starting transfers between devices, swap(): return lax.ppermute(values, axis, [(i, i ^ mask) for i in range(n)])  30.1 us
    ppermute x21, waiting for transfers between devices, swap(): return lax.ppermute(values, axis, [(i, i ^ mask) for i in range(n)])  23.8 us
    ppermute x3, starting transfers between devices, turn(): return lax.ppermute(values, BOTH, perm)  2.48 us
    unnamed x6, local copies, waits for them, and re-layouts  2.29 us
    pallas_call x1, Pallas kernels, per_device(): pl.pallas_call(functools.partial(update_kernel, inner_upper), out_shape=s...  2.15 us
    pallas_call x1, Pallas kernels, per_device(): pl.pallas_call(functools.partial(product_kernel, orders), out_shape=[shap...  1.77 us
  transfers between devices with their start and end apart: 24, of which 15 were waited for; matrix products, arithmetic and copies ran while one was open for 1% of the time, Pallas kernels for 6%

profile of v1, /device:TPU:0, one launch (start us, length us, event | category | flops | bytes accessed | tf_op | source)
XLA Modules:
  0.0 70.0 jit_solution(15673005832694811564)
XLA Ops:
  0.0 0.9 %slice_bitcast_fusion.2 = (f32[1,4,32,128]{3,2,1,0:T(8,128)S(1)}, f32[1,4,32,128]{3,2,1,0:T(8,128)S(1)}) fusion(f32[8,32,128]{2,1,0:T(8,128)} %bitcast.145), kind=kLoop, calls=%fused_computation.48 | loop fusion | bytes 262144 | tf_op jit(solution)/shard_map/broadcast_in_dim | solution.py:240
  0.9 4.1 %collective-permute-start.1 = (f32[1,4,32,128]{3,2,1,0:T(8,128)S(1)}, f32[1,4,32,128]{3,2,1,0:T(8,128)S(1)}, u32[]{:S(2)}, u32[]{:S(2)}) collective-permute-start(f32[1,4,32,128]{3,2,1,0:T(8,128)S(1)} %get-tuple-element.97), channel_id=1, source_target_pairs={{0,4},{1,5},{2,6},{3,7},{4,0},{5,1},{6,2},{7,3},{8,12},{9,13},{10,... | collective-permute-start | bytes 196616 | tf_op jit(solution)/shard_map/ppermute | solution.py:32
  5.0 0.1 collective-permute-start
  5.1 1.6 %copy-done = f32[8,1,128,4,1,128]{5,4,3,2,1,0:T(1,128)S(1)} copy-done((f32[8,1,128,4,1,128]{5,4,3,2,1,0:T(1,128)S(1)}, f32[8,1,128,4,1,128]{5,4,3,2,1,0:T(1,128)}, u32[]{:S(2)}) %copy-start) | copy-done | bytes 2097176
  6.7 0.8 %shard_map.37 = (bf16[1024,512]{1,0:T(8,128)(2,1)S(1)}, bf16[1024,512]{1,0:T(8,128)(2,1)S(1)}, f32[1024,512]{1,0:T(8,128)S(1)}) custom-call(f32[4096,128]{1,0:T(8,128)S(1)} %bitcast.134), custom_call_target="tpu_custom_call" | custom-call | flops 2097152 | bytes 4194304 | tf_op jit(solution)/shard_map/pallas_call | solution.py:232
  7.5 1.2 %collective-permute-done.1 = f32[1,4,32,128]{3,2,1,0:T(8,128)S(1)} collective-permute-done((f32[1,4,32,128]{3,2,1,0:T(8,128)S(1)}, f32[1,4,32,128]{3,2,1,0:T(8,128)S(1)}, u32[]{:S(2)}, u32[]{:S(2)}) %collective-permute-start.1) | collective-permute-done | bytes 65568 | tf_op jit(solution)/shard_map/ppermute | solution.py:32
  8.7 2.1 %collective-permute-start.2 = (f32[2,4,32,128]{3,2,1,0:T(8,128)S(1)}, f32[2,4,32,128]{3,2,1,0:T(8,128)S(1)}, u32[]{:S(2)}, u32[]{:S(2)}) collective-permute-start(f32[2,4,32,128]{3,2,1,0:T(8,128)S(1)} %maximum_bitcast_fusion.1), channel_id=1, source_target_pairs={{0,2},{1,3},{2,0},{3,1},{4,6},{5,7},{6,4},{7,5},{8,10},{9,11},{10,... | collective-permute-start | bytes 393224 | tf_op jit(solution)/shard_map/ppermute | solution.py:32
  10.8 0.6 collective-permute-done
  11.5 1.8 %collective-permute-start.4 = (f32[2,4,32,128]{3,2,1,0:T(8,128)S(1)}, f32[2,4,32,128]{3,2,1,0:T(8,128)S(1)}, u32[]{:S(2)}, u32[]{:S(2)}) collective-permute-start(f32[2,4,32,128]{3,2,1,0:T(8,128)S(1)} %maximum_bitcast_fusion.2), channel_id=1, source_target_pairs={{0,1},{1,0},{2,3},{3,2},{4,5},{5,4},{6,7},{7,6},{8,9},{9,8},{10,11... | collective-permute-start | bytes 393224 | tf_op jit(solution)/shard_map/ppermute | solution.py:32
  13.2 1.1 %collective-permute-done.2 = f32[2,4,32,128]{3,2,1,0:T(8,128)S(1)} collective-permute-done((f32[2,4,32,128]{3,2,1,0:T(8,128)S(1)}, f32[2,4,32,128]{3,2,1,0:T(8,128)S(1)}, u32[]{:S(2)}, u32[]{:S(2)}) %collective-permute-start.2) | collective-permute-done | bytes 131104 | tf_op jit(solution)/shard_map/ppermute | solution.py:32
  14.4 1.6 %collective-permute-start.3 = (f32[4,4,32,128]{3,2,1,0:T(8,128)S(1)}, f32[4,4,32,128]{3,2,1,0:T(8,128)S(1)}, u32[]{:S(2)}, u32[]{:S(2)}) collective-permute-start(f32[4,4,32,128]{3,2,1,0:T(8,128)S(1)} %bitcast.142), channel_id=1, source_target_pairs={{0,1},{1,0},{2,3},{3,2},{4,5},{5,4},{6,7},{7,6},{8,9},{9,8},{10,11... | collective-permute-start | bytes 786440 | tf_op jit(solution)/shard_map/ppermute | solution.py:32
  16.1 0.8 %collective-permute-done.4 = f32[2,4,32,128]{3,2,1,0:T(8,128)S(1)} collective-permute-done((f32[2,4,32,128]{3,2,1,0:T(8,128)S(1)}, f32[2,4,32,128]{3,2,1,0:T(8,128)S(1)}, u32[]{:S(2)}, u32[]{:S(2)}) %collective-permute-start.4) | collective-permute-done | bytes 131104 | tf_op jit(solution)/shard_map/ppermute | solution.py:32
  17.0 0.9 %collective-permute-start.5 = (f32[4,4,32,128]{3,2,1,0:T(8,128)S(1)}, f32[4,4,32,128]{3,2,1,0:T(8,128)S(1)}, u32[]{:S(2)}, u32[]{:S(2)}) collective-permute-start(f32[4,4,32,128]{3,2,1,0:T(8,128)S(1)} %bitcast.143), channel_id=1, source_target_pairs={{0,2},{1,3},{2,0},{3,1},{4,6},{5,7},{6,4},{7,5},{8,10},{9,11},{10,... | collective-permute-start | bytes 786440 | tf_op jit(solution)/shard_map/ppermute | solution.py:32
  17.9 4.5 %collective-permute-done.3 = f32[4,4,32,128]{3,2,1,0:T(8,128)S(1)} collective-permute-done((f32[4,4,32,128]{3,2,1,0:T(8,128)S(1)}, f32[4,4,32,128]{3,2,1,0:T(8,128)S(1)}, u32[]{:S(2)}, u32[]{:S(2)}) %collective-permute-start.3) | collective-permute-done | bytes 262176 | tf_op jit(solution)/shard_map/ppermute | solution.py:32
  22.3 1.6 %collective-permute-done.5 = f32[4,4,32,128]{3,2,1,0:T(8,128)S(1)} collective-permute-done((f32[4,4,32,128]{3,2,1,0:T(8,128)S(1)}, f32[4,4,32,128]{3,2,1,0:T(8,128)S(1)}, u32[]{:S(2)}, u32[]{:S(2)}) %collective-permute-start.5) | collective-permute-done | bytes 262176 | tf_op jit(solution)/shard_map/ppermute | solution.py:32
  23.9 0.1 select_bitcast_fusion.7
  24.2 0.0 copy-start.1
  24.2 1.8 %shard_map.38 = (f32[8,256,128]{2,1,0:T(8,128)S(1)}, f32[2,64,512]{2,1,0:T(8,128)S(1)}, f32[2,64,512]{2,1,0:T(8,128)}) custom-call(bf16[1024,512]{1,0:T(8,128)(2,1)S(1)} %get-tuple-element.43.ah_ref, bf16[1024,512]{1,0:T(8,128)(2,1)S(1)} %get-tuple-element.44.al_ref, f32[8,4,32,128]{3,2,1,0:T(8,128)S(1)} %bitcast.136, f32[8,4,32,128]{3,2,1,0:T(8,128)S(1)} %bitcast.135), custom_call_target="tpu_custom_call" | custom-call | flops 805306368 | bytes 4194304 | tf_op jit(solution)/shard_map/pallas_call | solution.py:247
  26.0 0.7 copy-done.2
  26.7 0.0 collective-permute-start.6
  26.7 1.9 %collective-permute-done.6 = f32[2,64,512]{2,1,0:T(8,128)} collective-permute-done((f32[2,64,512]{2,1,0:T(8,128)}, f32[2,64,512]{2,1,0:T(8,128)}, u32[]{:S(2)}, u32[]{:S(2)}) %collective-permute-start.6) | collective-permute-done | bytes 262176 | tf_op jit(solution)/shard_map/ppermute | solution.py:32
  28.5 1.1 %add.35 = f32[2,64,512]{2,1,0:T(8,128)S(1)} add(f32[2,64,512]{2,1,0:T(8,128)} %copy-done.2, f32[2,64,512]{2,1,0:T(8,128)} %collective-permute-done.6) | non-fusion elementwise | flops 65536 | bytes 786432 | tf_op jit(solution)/shard_map/add | solution.py:257
  29.6 1.2 %collective-permute-start.8 = (f32[64,512]{1,0:T(8,128)S(1)}, f32[64,512]{1,0:T(8,128)S(1)}, u32[]{:S(2)}, u32[]{:S(2)}) collective-permute-start(f32[64,512]{1,0:T(8,128)S(1)} %get-tuple-element.81), channel_id=1, source_target_pairs={{0,2},{1,10},{2,18},{3,26},{4,6},{5,14},{6,22},{7,30},{8,3},{9,11}... | collective-permute-start | bytes 393224 | tf_op jit(solution)/shard_map/ppermute | solution.py:227
  30.8 0.7 collective-permute-start.7
  31.5 0.0 copy-done.1
  31.5 1.0 %shard_map.39.ur_ref = bf16[1024,768]{1,0:T(8,128)(2,1)S(1)} custom-call(f32[256,256]{1,0:T(8,128)S(1)} %copy-done.1, f32[8,256,128]{2,1,0:T(8,128)S(1)} %get-tuple-element.66.y_ref), custom_call_target="tpu_custom_call" | custom-call | flops 402653184 | bytes 2097152 | tf_op jit(solution)/shard_map/pallas_call | solution.py:276
  32.6 4.3 %collective-permute-start.10 = (f32[1,64,512]{2,1,0:T(8,128)S(1)}, f32[1,64,512]{2,1,0:T(8,128)S(1)}, u32[]{:S(2)}, u32[]{:S(2)}) collective-permute-start(f32[1,64,512]{2,1,0:T(8,128)S(1)} %constant_dynamic-slice_fusion), channel_id=1, source_target_pairs={{0,16},{8,24},{16,0},{24,8},{1,17},{9,25},{17,1},{25,9},{2,18},{10... | collective-permute-start | bytes 393224 | tf_op jit(solution)/shard_map/ppermute | solution.py:32
  36.8 0.7 collective-permute-start.11
  37.5 0.0 collective-permute-done.8
  37.5 0.0 collective-permute-done.7
  37.6 3.4 %collective-permute-start.9 = (f32[1,32,512]{2,1,0:T(8,128)S(1)}, f32[1,32,512]{2,1,0:T(8,128)S(1)}, u32[]{:S(2)}, u32[]{:S(2)}) collective-permute-start(f32[1,32,512]{2,1,0:T(8,128)S(1)} %get-tuple-element.90), channel_id=1, source_target_pairs={{0,4},{1,5},{2,6},{3,7},{4,0},{5,1},{6,2},{7,3},{8,12},{9,13},{10,... | collective-permute-start | bytes 196616 | tf_op jit(solution)/shard_map/ppermute | solution.py:32
  41.0 0.1 collective-permute-start.16
  41.1 3.6 %collective-permute-done.10 = f32[1,64,512]{2,1,0:T(8,128)S(1)} collective-permute-done((f32[1,64,512]{2,1,0:T(8,128)S(1)}, f32[1,64,512]{2,1,0:T(8,128)S(1)}, u32[]{:S(2)}, u32[]{:S(2)}) %collective-permute-start.10) | collective-permute-done | bytes 131104 | tf_op jit(solution)/shard_map/ppermute | solution.py:32
  44.8 0.0 collective-permute-done.11
  44.8 0.0 collective-permute-done.9
  44.9 4.2 %collective-permute-start.14 = (f32[2,32,512]{2,1,0:T(8,128)S(1)}, f32[2,32,512]{2,1,0:T(8,128)S(1)}, u32[]{:S(2)}, u32[]{:S(2)}) collective-permute-start(f32[2,32,512]{2,1,0:T(8,128)S(1)} %maximum_bitcast_fusion.3.first_ref), channel_id=1, source_target_pairs={{0,2},{1,3},{2,0},{3,1},{4,6},{5,7},{6,4},{7,5},{8,10},{9,11},{10,... | collective-permute-start | bytes 393224 | tf_op jit(solution)/shard_map/ppermute | solution.py:32
  49.0 0.0 collective-permute-done.16
  49.1 1.4 %collective-permute-start.17 = (f32[2,32,512]{2,1,0:T(8,128)S(1)}, f32[2,32,512]{2,1,0:T(8,128)S(1)}, u32[]{:S(2)}, u32[]{:S(2)}) collective-permute-start(f32[2,32,512]{2,1,0:T(8,128)S(1)} %maximum_bitcast_fusion.4.second_ref), channel_id=1, source_target_pairs={{0,1},{1,0},{2,3},{3,2},{4,5},{5,4},{6,7},{7,6},{8,9},{9,8},{10,11... | collective-permute-start | bytes 393224 | tf_op jit(solution)/shard_map/ppermute | solution.py:32
  50.5 0.5 collective-permute-start.12
  50.9 2.4 %collective-permute-done.14 = f32[2,32,512]{2,1,0:T(8,128)S(1)} collective-permute-done((f32[2,32,512]{2,1,0:T(8,128)S(1)}, f32[2,32,512]{2,1,0:T(8,128)S(1)}, u32[]{:S(2)}, u32[]{:S(2)}) %collective-permute-start.14) | collective-permute-done | bytes 131104 | tf_op jit(solution)/shard_map/ppermute | solution.py:32
  53.4 0.7 shard_map.42
  54.1 0.1 collective-permute-start.19
  54.2 0.1 collective-permute-start.15
  54.2 0.8 %collective-permute-done.17 = f32[2,32,512]{2,1,0:T(8,128)S(1)} collective-permute-done((f32[2,32,512]{2,1,0:T(8,128)S(1)}, f32[2,32,512]{2,1,0:T(8,128)S(1)}, u32[]{:S(2)}, u32[]{:S(2)}) %collective-permute-start.17) | collective-permute-done | bytes 131104 | tf_op jit(solution)/shard_map/ppermute | solution.py:32
  55.1 1.1 %collective-permute-start.18 = (f32[4,32,512]{2,1,0:T(8,128)S(1)}, f32[4,32,512]{2,1,0:T(8,128)S(1)}, u32[]{:S(2)}, u32[]{:S(2)}) collective-permute-start(f32[4,32,512]{2,1,0:T(8,128)S(1)} %bitcast.137), channel_id=1, source_target_pairs={{0,2},{1,3},{2,0},{3,1},{4,6},{5,7},{6,4},{7,5},{8,10},{9,11},{10,... | collective-permute-start | bytes 786440 | tf_op jit(solution)/shard_map/ppermute | solution.py:32
  56.2 0.0 collective-permute-done.19
  56.3 0.8 %collective-permute-start.20 = (f32[32,512]{1,0:T(8,128)S(1)}, f32[32,512]{1,0:T(8,128)S(1)}, u32[]{:S(2)}, u32[]{:S(2)}) collective-permute-start(f32[32,512]{1,0:T(8,128)S(1)} %add.44), channel_id=1, source_target_pairs={{0,16},{8,24},{16,0},{24,8},{1,17},{9,25},{17,1},{25,9},{2,18},{10... | collective-permute-start | bytes 196616 | tf_op jit(solution)/shard_map/ppermute | solution.py:32
  57.1 1.9 %collective-permute-done.12 = f32[1,4,32,512]{3,2,1,0:T(8,128)S(1)} collective-permute-done((f32[1,4,32,512]{3,2,1,0:T(8,128)S(1)}, f32[1,4,32,512]{3,2,1,0:T(8,128)S(1)}, u32[]{:S(2)}, u32[]{:S(2)}) %collective-permute-start.12) | collective-permute-done | bytes 262176 | tf_op jit(solution)/shard_map/ppermute | solution.py:32
  59.1 0.1 collective-permute-start.13
  59.2 1.4 %collective-permute-done.20 = f32[32,512]{1,0:T(8,128)S(1)} collective-permute-done((f32[32,512]{1,0:T(8,128)S(1)}, f32[32,512]{1,0:T(8,128)S(1)}, u32[]{:S(2)}, u32[]{:S(2)}) %collective-permute-start.20) | collective-permute-done | bytes 65568 | tf_op jit(solution)/shard_map/ppermute | solution.py:32
  60.6 1.7 %collective-permute-start.23 = (f32[1,32,512]{2,1,0:T(8,128)S(1)}, f32[1,32,512]{2,1,0:T(8,128)S(1)}, u32[]{:S(2)}, u32[]{:S(2)}) collective-permute-start(f32[1,32,512]{2,1,0:T(8,128)S(1)} %add_bitcast_fusion.refs_0_), channel_id=1, source_target_pairs={{0,3},{1,2},{2,1},{3,0},{4,7},{5,6},{6,5},{7,4},{8,11},{9,10},{10,... | collective-permute-start | bytes 196616 | tf_op jit(solution)/shard_map/ppermute | solution.py:32
  62.3 1.3 %collective-permute-start.22 = (f32[1,32,512]{2,1,0:T(8,128)S(1)}, f32[1,32,512]{2,1,0:T(8,128)S(1)}, u32[]{:S(2)}, u32[]{:S(2)}) collective-permute-start(f32[1,32,512]{2,1,0:T(8,128)S(1)} %add_bitcast_fusion.refs_0_), channel_id=1, source_target_pairs={{0,2},{1,3},{2,0},{3,1},{4,6},{5,7},{6,4},{7,5},{8,10},{9,11},{10,... | collective-permute-start | bytes 196616 | tf_op jit(solution)/shard_map/ppermute | solution.py:32
  63.6 0.0 collective-permute-done.15
  63.6 0.6 collective-permute-start.21
  64.3 0.0 collective-permute-done.13
  64.3 0.1 select_bitcast_fusion.1
  64.4 0.1 pad_maximum_fusion
  64.5 0.4 shard_map.40
  64.9 0.0 collective-permute-done.18.came_ref
  64.9 1.1 %shard_map.41.rest_ref = f32[1024,512]{1,0:T(8,128)S(1)} custom-call(f32[1024,512]{1,0:T(8,128)S(1)} %get-tuple-element.36.a_ref, bf16[768,512]{1,0:T(8,128)(2,1)S(1)} %get-tuple-element.61.uc_ref, f32[8,32,512]{2,1,0:T(8,128)S(1)} %bitcast.133, f32[4,32,512]{2,1,0:T(8,128)S(1)} %bitcast.138, f32[4,32,512]{2,1,0:T(8,128)S(1)} %collective-permute-done.18.came_ref), custom_call_target="tpu_custom_call" | custom-call | flops 805306368 | bytes 4194304 | tf_op jit(solution)/shard_map/pallas_call | solution.py:328
  66.1 0.3 collective-permute-done.23.refs_3_
  66.4 0.4 collective-permute-done.22.refs_2_
  66.8 1.1 %collective-permute-done.21.refs_1_ = f32[1,32,512]{2,1,0:T(8,128)S(1)} collective-permute-done((f32[1,32,512]{2,1,0:T(8,128)S(1)}, f32[1,32,512]{2,1,0:T(8,128)S(1)}, u32[]{:S(2)}, u32[]{:S(2)}) %collective-permute-start.21) | collective-permute-done | bytes 65568 | tf_op jit(solution)/shard_map/ppermute | solution.py:32
  67.9 2.2 %shard_map.43 = f32[4096,128]{1,0:T(8,128)} custom-call(f32[1024,512]{1,0:T(8,128)S(1)} %shard_map.41.rest_ref, bf16[1024,768]{1,0:T(8,128)(2,1)S(1)} %shard_map.39.ur_ref, bf16[768,512]{1,0:T(8,128)(2,1)S(1)} %get-tuple-element.61.uc_ref, f32[256,512]{1,0:T(8,128)S(1)} %get-tuple-element.65.zc_ref, f32[1,32,512]{2,1,0:T(8,128)S(1)} %add_bitcast_fusion.refs_0_, ...), custom_call_target="tpu_custom_call" | custom-call | flops 805306368 | bytes 4194304 | tf_op jit(solution)/shard_map/pallas_call | solution.py:339
  (33 shorter events, 0.7 us)
Async XLA Ops:
  0.9 7.8 %collective-permute-start.1 = (f32[1,4,32,128]{3,2,1,0:T(8,128)S(1)}, f32[1,4,32,128]{3,2,1,0:T(8,128)S(1)}, u32[]{:S(2)}, u32[]{:S(2)}) collective-permute-start(f32[1,4,32,128]{3,2,1,0:T(8,128)S(1)} %get-tuple-element.97), channel_id=1, source_target_pairs={{0,4},{1,5},{2,6},{3,7},{4,0},{5,1},{6,2},{7,3},{8,12},{9,13},{10,... | collective-permute-start | bytes 196616 | tf_op jit(solution)/shard_map/ppermute | solution.py:32
  5.0 6.5 %collective-permute-start = (f32[1,4,32,128]{3,2,1,0:T(8,128)S(1)}, f32[1,4,32,128]{3,2,1,0:T(8,128)S(1)}, u32[]{:S(2)}, u32[]{:S(2)}) collective-permute-start(f32[1,4,32,128]{3,2,1,0:T(8,128)S(1)} %get-tuple-element.98), channel_id=1, source_target_pairs={{0,4},{1,5},{2,6},{3,7},{4,0},{5,1},{6,2},{7,3},{8,12},{9,13},{10,... | collective-permute-start | bytes 196616 | tf_op jit(solution)/shard_map/ppermute | solution.py:32
  5.1 1.6 %copy-start = (f32[8,1,128,4,1,128]{5,4,3,2,1,0:T(1,128)S(1)}, f32[8,1,128,4,1,128]{5,4,3,2,1,0:T(1,128)}, u32[]{:S(2)}) copy-start(f32[8,1,128,4,1,128]{5,4,3,2,1,0:T(1,128)} %param.3) | copy-start | bytes 6291460
  8.7 5.7 %collective-permute-start.2 = (f32[2,4,32,128]{3,2,1,0:T(8,128)S(1)}, f32[2,4,32,128]{3,2,1,0:T(8,128)S(1)}, u32[]{:S(2)}, u32[]{:S(2)}) collective-permute-start(f32[2,4,32,128]{3,2,1,0:T(8,128)S(1)} %maximum_bitcast_fusion.1), channel_id=1, source_target_pairs={{0,2},{1,3},{2,0},{3,1},{4,6},{5,7},{6,4},{7,5},{8,10},{9,11},{10,... | collective-permute-start | bytes 393224 | tf_op jit(solution)/shard_map/ppermute | solution.py:32
  11.5 5.4 %collective-permute-start.4 = (f32[2,4,32,128]{3,2,1,0:T(8,128)S(1)}, f32[2,4,32,128]{3,2,1,0:T(8,128)S(1)}, u32[]{:S(2)}, u32[]{:S(2)}) collective-permute-start(f32[2,4,32,128]{3,2,1,0:T(8,128)S(1)} %maximum_bitcast_fusion.2), channel_id=1, source_target_pairs={{0,1},{1,0},{2,3},{3,2},{4,5},{5,4},{6,7},{7,6},{8,9},{9,8},{10,11... | collective-permute-start | bytes 393224 | tf_op jit(solution)/shard_map/ppermute | solution.py:32
  14.4 7.9 %collective-permute-start.3 = (f32[4,4,32,128]{3,2,1,0:T(8,128)S(1)}, f32[4,4,32,128]{3,2,1,0:T(8,128)S(1)}, u32[]{:S(2)}, u32[]{:S(2)}) collective-permute-start(f32[4,4,32,128]{3,2,1,0:T(8,128)S(1)} %bitcast.142), channel_id=1, source_target_pairs={{0,1},{1,0},{2,3},{3,2},{4,5},{5,4},{6,7},{7,6},{8,9},{9,8},{10,11... | collective-permute-start | bytes 786440 | tf_op jit(solution)/shard_map/ppermute | solution.py:32
  17.0 7.0 %collective-permute-start.5 = (f32[4,4,32,128]{3,2,1,0:T(8,128)S(1)}, f32[4,4,32,128]{3,2,1,0:T(8,128)S(1)}, u32[]{:S(2)}, u32[]{:S(2)}) collective-permute-start(f32[4,4,32,128]{3,2,1,0:T(8,128)S(1)} %bitcast.143), channel_id=1, source_target_pairs={{0,2},{1,3},{2,0},{3,1},{4,6},{5,7},{6,4},{7,5},{8,10},{9,11},{10,... | collective-permute-start | bytes 786440 | tf_op jit(solution)/shard_map/ppermute | solution.py:32
  24.2 7.3 %copy-start.1 = (f32[256,256]{1,0:T(8,128)S(1)}, f32[256,256]{1,0:T(8,128)}, u32[]{:S(2)}) copy-start(f32[256,256]{1,0:T(8,128)} %t_ref.3) | copy-start | bytes 786436
  26.0 0.7 copy-start.2
  26.7 1.9 %collective-permute-start.6 = (f32[2,64,512]{2,1,0:T(8,128)}, f32[2,64,512]{2,1,0:T(8,128)}, u32[]{:S(2)}, u32[]{:S(2)}) collective-permute-start(f32[2,64,512]{2,1,0:T(8,128)} %get-tuple-element.49), channel_id=1, source_target_pairs={{0,8},{8,0},{16,24},{24,16},{1,9},{9,1},{17,25},{25,17},{2,10},{10... | collective-permute-start | bytes 786440 | tf_op jit(solution)/shard_map/ppermute | solution.py:32
  29.6 7.9 %collective-permute-start.8 = (f32[64,512]{1,0:T(8,128)S(1)}, f32[64,512]{1,0:T(8,128)S(1)}, u32[]{:S(2)}, u32[]{:S(2)}) collective-permute-start(f32[64,512]{1,0:T(8,128)S(1)} %get-tuple-element.81), channel_id=1, source_target_pairs={{0,2},{1,10},{2,18},{3,26},{4,6},{5,14},{6,22},{7,30},{8,3},{9,11}... | collective-permute-start | bytes 393224 | tf_op jit(solution)/shard_map/ppermute | solution.py:227
  30.8 6.7 %collective-permute-start.7 = (f32[64,512]{1,0:T(8,128)S(1)}, f32[64,512]{1,0:T(8,128)S(1)}, u32[]{:S(2)}, u32[]{:S(2)}) collective-permute-start(f32[64,512]{1,0:T(8,128)S(1)} %get-tuple-element.82), channel_id=1, source_target_pairs={{0,0},{1,8},{2,16},{3,24},{4,4},{5,12},{6,20},{7,28},{8,1},{9,9},{... | collective-permute-start | bytes 393224 | tf_op jit(solution)/shard_map/ppermute | solution.py:227
  32.6 12.2 %collective-permute-start.10 = (f32[1,64,512]{2,1,0:T(8,128)S(1)}, f32[1,64,512]{2,1,0:T(8,128)S(1)}, u32[]{:S(2)}, u32[]{:S(2)}) collective-permute-start(f32[1,64,512]{2,1,0:T(8,128)S(1)} %constant_dynamic-slice_fusion), channel_id=1, source_target_pairs={{0,16},{8,24},{16,0},{24,8},{1,17},{9,25},{17,1},{25,9},{2,18},{10... | collective-permute-start | bytes 393224 | tf_op jit(solution)/shard_map/ppermute | solution.py:32
  36.8 7.9 %collective-permute-start.11 = (f32[64,512]{1,0:T(8,128)S(1)}, f32[64,512]{1,0:T(8,128)S(1)}, u32[]{:S(2)}, u32[]{:S(2)}) collective-permute-start(f32[64,512]{1,0:T(8,128)S(1)} %copy_bitcast_fusion), channel_id=1, source_target_pairs={{0,0},{1,8},{2,16},{3,24},{4,4},{5,12},{6,20},{7,28},{8,1},{9,9},{... | collective-permute-start | bytes 393224 | tf_op jit(solution)/shard_map/ppermute | solution.py:227
  37.6 7.2 %collective-permute-start.9 = (f32[1,32,512]{2,1,0:T(8,128)S(1)}, f32[1,32,512]{2,1,0:T(8,128)S(1)}, u32[]{:S(2)}, u32[]{:S(2)}) collective-permute-start(f32[1,32,512]{2,1,0:T(8,128)S(1)} %get-tuple-element.90), channel_id=1, source_target_pairs={{0,4},{1,5},{2,6},{3,7},{4,0},{5,1},{6,2},{7,3},{8,12},{9,13},{10,... | collective-permute-start | bytes 196616 | tf_op jit(solution)/shard_map/ppermute | solution.py:32
  41.0 8.0 %collective-permute-start.16 = (f32[1,32,512]{2,1,0:T(8,128)S(1)}, f32[1,32,512]{2,1,0:T(8,128)S(1)}, u32[]{:S(2)}, u32[]{:S(2)}) collective-permute-start(f32[1,32,512]{2,1,0:T(8,128)S(1)} %get-tuple-element.89), channel_id=1, source_target_pairs={{0,4},{1,5},{2,6},{3,7},{4,0},{5,1},{6,2},{7,3},{8,12},{9,13},{10,... | collective-permute-start | bytes 196616 | tf_op jit(solution)/shard_map/ppermute | solution.py:32
  44.9 8.5 %collective-permute-start.14 = (f32[2,32,512]{2,1,0:T(8,128)S(1)}, f32[2,32,512]{2,1,0:T(8,128)S(1)}, u32[]{:S(2)}, u32[]{:S(2)}) collective-permute-start(f32[2,32,512]{2,1,0:T(8,128)S(1)} %maximum_bitcast_fusion.3.first_ref), channel_id=1, source_target_pairs={{0,2},{1,3},{2,0},{3,1},{4,6},{5,7},{6,4},{7,5},{8,10},{9,11},{10,... | collective-permute-start | bytes 393224 | tf_op jit(solution)/shard_map/ppermute | solution.py:32
  49.1 6.0 %collective-permute-start.17 = (f32[2,32,512]{2,1,0:T(8,128)S(1)}, f32[2,32,512]{2,1,0:T(8,128)S(1)}, u32[]{:S(2)}, u32[]{:S(2)}) collective-permute-start(f32[2,32,512]{2,1,0:T(8,128)S(1)} %maximum_bitcast_fusion.4.second_ref), channel_id=1, source_target_pairs={{0,1},{1,0},{2,3},{3,2},{4,5},{5,4},{6,7},{7,6},{8,9},{9,8},{10,11... | collective-permute-start | bytes 393224 | tf_op jit(solution)/shard_map/ppermute | solution.py:32
  50.5 8.5 %collective-permute-start.12 = (f32[1,4,32,512]{3,2,1,0:T(8,128)S(1)}, f32[1,4,32,512]{3,2,1,0:T(8,128)S(1)}, u32[]{:S(2)}, u32[]{:S(2)}) collective-permute-start(f32[1,4,32,512]{3,2,1,0:T(8,128)S(1)} %bitcast.139), channel_id=1, source_target_pairs={{0,16},{8,24},{16,0},{24,8},{1,17},{9,25},{17,1},{25,9},{2,18},{10... | collective-permute-start | bytes 786440 | tf_op jit(solution)/shard_map/ppermute | solution.py:32
  54.1 2.2 %collective-permute-start.19 = (f32[32,512]{1,0:T(8,128)S(1)}, f32[32,512]{1,0:T(8,128)S(1)}, u32[]{:S(2)}, u32[]{:S(2)}) collective-permute-start(f32[32,512]{1,0:T(8,128)S(1)} %shard_map.42), channel_id=1, source_target_pairs={{0,8},{8,0},{16,24},{24,16},{1,9},{9,1},{17,25},{25,17},{2,10},{10... | collective-permute-start | bytes 196616 | tf_op jit(solution)/shard_map/ppermute | solution.py:32
  54.2 9.5 %collective-permute-start.15 = (f32[4,32,512]{2,1,0:T(8,128)S(1)}, f32[4,32,512]{2,1,0:T(8,128)S(1)}, u32[]{:S(2)}, u32[]{:S(2)}) collective-permute-start(f32[4,32,512]{2,1,0:T(8,128)S(1)} %bitcast.140), channel_id=1, source_target_pairs={{0,1},{1,0},{2,3},{3,2},{4,5},{5,4},{6,7},{7,6},{8,9},{9,8},{10,11... | collective-permute-start | bytes 786440 | tf_op jit(solution)/shard_map/ppermute | solution.py:32
  55.1 9.8 %collective-permute-start.18 = (f32[4,32,512]{2,1,0:T(8,128)S(1)}, f32[4,32,512]{2,1,0:T(8,128)S(1)}, u32[]{:S(2)}, u32[]{:S(2)}) collective-permute-start(f32[4,32,512]{2,1,0:T(8,128)S(1)} %bitcast.137), channel_id=1, source_target_pairs={{0,2},{1,3},{2,0},{3,1},{4,6},{5,7},{6,4},{7,5},{8,10},{9,11},{10,... | collective-permute-start | bytes 786440 | tf_op jit(solution)/shard_map/ppermute | solution.py:32
  56.3 4.3 %collective-permute-start.20 = (f32[32,512]{1,0:T(8,128)S(1)}, f32[32,512]{1,0:T(8,128)S(1)}, u32[]{:S(2)}, u32[]{:S(2)}) collective-permute-start(f32[32,512]{1,0:T(8,128)S(1)} %add.44), channel_id=1, source_target_pairs={{0,16},{8,24},{16,0},{24,8},{1,17},{9,25},{17,1},{25,9},{2,18},{10... | collective-permute-start | bytes 196616 | tf_op jit(solution)/shard_map/ppermute | solution.py:32
  59.1 5.2 %collective-permute-start.13 = (f32[2,4,32,512]{3,2,1,0:T(8,128)S(1)}, f32[2,4,32,512]{3,2,1,0:T(8,128)S(1)}, u32[]{:S(2)}, u32[]{:S(2)}) collective-permute-start(f32[2,4,32,512]{3,2,1,0:T(8,128)S(1)} %maximum_bitcast_fusion), channel_id=1, source_target_pairs={{0,8},{8,0},{16,24},{24,16},{1,9},{9,1},{17,25},{25,17},{2,10},{10... | collective-permute-start | bytes 1572872 | tf_op jit(solution)/shard_map/ppermute | solution.py:32
  60.6 5.8 %collective-permute-start.23 = (f32[1,32,512]{2,1,0:T(8,128)S(1)}, f32[1,32,512]{2,1,0:T(8,128)S(1)}, u32[]{:S(2)}, u32[]{:S(2)}) collective-permute-start(f32[1,32,512]{2,1,0:T(8,128)S(1)} %add_bitcast_fusion.refs_0_), channel_id=1, source_target_pairs={{0,3},{1,2},{2,1},{3,0},{4,7},{5,6},{6,5},{7,4},{8,11},{9,10},{10,... | collective-permute-start | bytes 196616 | tf_op jit(solution)/shard_map/ppermute | solution.py:32
  62.3 4.4 %collective-permute-start.22 = (f32[1,32,512]{2,1,0:T(8,128)S(1)}, f32[1,32,512]{2,1,0:T(8,128)S(1)}, u32[]{:S(2)}, u32[]{:S(2)}) collective-permute-start(f32[1,32,512]{2,1,0:T(8,128)S(1)} %add_bitcast_fusion.refs_0_), channel_id=1, source_target_pairs={{0,2},{1,3},{2,0},{3,1},{4,6},{5,7},{6,4},{7,5},{8,10},{9,11},{10,... | collective-permute-start | bytes 196616 | tf_op jit(solution)/shard_map/ppermute | solution.py:32
  63.6 4.3 %collective-permute-start.21 = (f32[1,32,512]{2,1,0:T(8,128)S(1)}, f32[1,32,512]{2,1,0:T(8,128)S(1)}, u32[]{:S(2)}, u32[]{:S(2)}) collective-permute-start(f32[1,32,512]{2,1,0:T(8,128)S(1)} %add_bitcast_fusion.refs_0_), channel_id=1, source_target_pairs={{0,1},{1,0},{2,3},{3,2},{4,5},{5,4},{6,7},{7,6},{8,9},{9,8},{10,11... | collective-permute-start | bytes 196616 | tf_op jit(solution)/shard_map/ppermute | solution.py:32

commit v2 on v1

--- a/solution.py
+++ b/solution.py
@@ -38,6 +38,11 @@
         n //= 2
         masks.append(n)
     return masks
+
+
+def pick(values, index):
+    start = (index,) + (jnp.uint32(0),) * (values.ndim - 1)
+    return lax.dynamic_slice(values, start, (1,) + values.shape[1:])[0]
 
 
 def join(values, other, high):
@@ -206,12 +211,12 @@
     prow, pcol = lax.axis_index("prow").astype(jnp.int32), lax.axis_index("pcol").astype(jnp.int32)
     group = pcol >> shift
     where = {
-        "group": group,
-        "rounds": [(prow >> 1) ^ r for r in range(ny)],
-        "share": (pcol & (np_ - 1)) * part,
+        "group": group.astype(jnp.uint32),
+        "rounds": [((prow >> 1) ^ r).astype(jnp.uint32) for r in range(ny)],
+        "share": ((pcol & (np_ - 1)) * part).astype(jnp.uint32),
         "col": {mask: (pcol & mask) != 0 for mask in masks},
         "row": {mask: (prow & mask) != 0 for mask in cols_order},
-        "half": {mask: [jnp.where((prow & mask) != 0, 1 - side, side) for side in range(2)] for mask in cols_order},
+        "half": {mask: [((prow >> (mask.bit_length() - 1) & 1) ^ side).astype(jnp.uint32) for side in range(2)] for mask in cols_order},
     }
     mine, where = lax.optimization_barrier((mine, where))
     group, col, row = where["group"], where["col"], where["row"]
@@ -255,22 +260,23 @@
     )(a_high, a_low, first, second)
     other = swap(send, "prow", 1)
     kept = keep + other
+    zero = jnp.uint32(0)
     y_piece = lax.dynamic_slice(
-        y_rows.reshape(col_tiles, ratio, nb, tile), (0, group, where["share"], 0), (col_tiles, 1, part, tile)
+        y_rows.reshape(col_tiles, ratio, nb, tile), (zero, group, where["share"], zero), (col_tiles, 1, part, tile)
     )
     y_piece = jnp.transpose(y_piece.reshape(col_tiles, part, tile), (1, 0, 2)).reshape(part, cols)
 
     turned = []
     for r in range(ny):
-        message = lax.dynamic_index_in_dim(kept, where["rounds"][r], 0, keepdims=False)
+        message = pick(kept, where["rounds"][r])
         turned.append(turn(message, 2 * r))
     turned = sum(turned[1:], turned[0])
     y_piece, kept = lax.optimization_barrier((y_piece, kept))
     for mask in cols_order[:-1]:
         low, high = where["half"][mask]
         pair = kept.reshape(2, mask // 2, part, cols)
-        kept = lax.dynamic_index_in_dim(pair, low, 0, keepdims=False)
-        kept = kept + swap(lax.dynamic_index_in_dim(pair, high, 0, keepdims=False), "prow", mask)
+        kept = pick(pair, low)
+        kept = kept + swap(pick(pair, high), "prow", mask)
     piece = kept.reshape(part, cols)
     y_cols = turn(y_piece, 0).reshape(2, part // 2, cols)
     u_rows = pl.pallas_call(

time: 70.3 us -> 67.5 us (0.960)
  other arithmetic: 1.99 us -> 0.94 us
  Pallas kernels: 7.96 us -> 7.22 us
    add x1, other arithmetic: 1.06 us -> 0.04 us  [per_device(): kept = keep + other]
    pallas_call x1, Pallas kernels: 1.77 us -> 1.05 us  [per_device(): pl.pallas_call(functools.partial(product_kernel, orders), out_shape=[shap...]
    unnamed x6 -> x4, local copies, waits for them, and re-layouts: 2.29 us -> 1.6 us
where the time goes in v2:
time: 67.5 us; the launch traced here: 67.3 us
  starting transfers between devices  32.7 us (48%)
  waiting for transfers between devices  23.5 us (35%)
  Pallas kernels  7.22 us (11%)
  local copies, waits for them, and re-layouts  2.55 us (4%)
  other arithmetic  0.94 us (1%)
    ppermute x21, starting transfers between devices, swap(): return lax.ppermute(values, axis, [(i, i ^ mask) for i in range(n)])  30.2 us
    ppermute x21, waiting for transfers between devices, swap(): return lax.ppermute(values, axis, [(i, i ^ mask) for i in range(n)])  23.5 us
    ppermute x3, starting transfers between devices, turn(): return lax.ppermute(values, BOTH, perm)  2.46 us
    pallas_call x1, Pallas kernels, per_device(): pl.pallas_call(functools.partial(update_kernel, inner_upper), out_shape=s...  2.15 us
    unnamed x4, local copies, waits for them, and re-layouts  1.6 us
  transfers between devices with their start and end apart: 24, of which 15 were waited for; matrix products, arithmetic and copies ran while one was open for 1% of the time, Pallas kernels for 6%

profile of v2, /device:TPU:0, one launch (start us, length us, event | category | flops | bytes accessed | tf_op | source)
XLA Modules:
  0.0 67.3 jit_solution(9091474463560413504)
XLA Ops:
  0.0 0.9 %slice_bitcast_fusion.2 = (f32[1,4,32,128]{3,2,1,0:T(8,128)S(1)}, f32[1,4,32,128]{3,2,1,0:T(8,128)S(1)}) fusion(f32[8,32,128]{2,1,0:T(8,128)} %bitcast.145), kind=kLoop, calls=%fused_computation.48 | loop fusion | bytes 262144 | tf_op jit(solution)/shard_map/broadcast_in_dim | solution.py:245
  0.9 4.1 %collective-permute-start.1 = (f32[1,4,32,128]{3,2,1,0:T(8,128)S(1)}, f32[1,4,32,128]{3,2,1,0:T(8,128)S(1)}, u32[]{:S(2)}, u32[]{:S(2)}) collective-permute-start(f32[1,4,32,128]{3,2,1,0:T(8,128)S(1)} %get-tuple-element.97), channel_id=1, source_target_pairs={{0,4},{1,5},{2,6},{3,7},{4,0},{5,1},{6,2},{7,3},{8,12},{9,13},{10,... | collective-permute-start | bytes 196616 | tf_op jit(solution)/shard_map/ppermute | solution.py:32
  5.0 0.1 collective-permute-start
  5.1 0.0 copy-start
  5.1 1.6 %copy-done = f32[8,1,128,4,1,128]{5,4,3,2,1,0:T(1,128)S(1)} copy-done((f32[8,1,128,4,1,128]{5,4,3,2,1,0:T(1,128)S(1)}, f32[8,1,128,4,1,128]{5,4,3,2,1,0:T(1,128)}, u32[]{:S(2)}) %copy-start) | copy-done | bytes 2097176
  6.7 0.8 %shard_map.37 = (bf16[1024,512]{1,0:T(8,128)(2,1)S(1)}, bf16[1024,512]{1,0:T(8,128)(2,1)S(1)}, f32[1024,512]{1,0:T(8,128)S(1)}) custom-call(f32[4096,128]{1,0:T(8,128)S(1)} %bitcast.134), custom_call_target="tpu_custom_call" | custom-call | flops 2097152 | bytes 4194304 | tf_op jit(solution)/shard_map/pallas_call | solution.py:237
  7.5 1.2 %collective-permute-done.1 = f32[1,4,32,128]{3,2,1,0:T(8,128)S(1)} collective-permute-done((f32[1,4,32,128]{3,2,1,0:T(8,128)S(1)}, f32[1,4,32,128]{3,2,1,0:T(8,128)S(1)}, u32[]{:S(2)}, u32[]{:S(2)}) %collective-permute-start.1) | collective-permute-done | bytes 65568 | tf_op jit(solution)/shard_map/ppermute | solution.py:32
  8.7 2.1 %collective-permute-start.2 = (f32[2,4,32,128]{3,2,1,0:T(8,128)S(1)}, f32[2,4,32,128]{3,2,1,0:T(8,128)S(1)}, u32[]{:S(2)}, u32[]{:S(2)}) collective-permute-start(f32[2,4,32,128]{3,2,1,0:T(8,128)S(1)} %maximum_bitcast_fusion.1), channel_id=1, source_target_pairs={{0,2},{1,3},{2,0},{3,1},{4,6},{5,7},{6,4},{7,5},{8,10},{9,11},{10,... | collective-permute-start | bytes 393224 | tf_op jit(solution)/shard_map/ppermute | solution.py:32
  10.8 0.6 collective-permute-done
  11.5 1.8 %collective-permute-start.4 = (f32[2,4,32,128]{3,2,1,0:T(8,128)S(1)}, f32[2,4,32,128]{3,2,1,0:T(8,128)S(1)}, u32[]{:S(2)}, u32[]{:S(2)}) collective-permute-start(f32[2,4,32,128]{3,2,1,0:T(8,128)S(1)} %maximum_bitcast_fusion.2), channel_id=1, source_target_pairs={{0,1},{1,0},{2,3},{3,2},{4,5},{5,4},{6,7},{7,6},{8,9},{9,8},{10,11... | collective-permute-start | bytes 393224 | tf_op jit(solution)/shard_map/ppermute | solution.py:32
  13.2 1.1 %collective-permute-done.2 = f32[2,4,32,128]{3,2,1,0:T(8,128)S(1)} collective-permute-done((f32[2,4,32,128]{3,2,1,0:T(8,128)S(1)}, f32[2,4,32,128]{3,2,1,0:T(8,128)S(1)}, u32[]{:S(2)}, u32[]{:S(2)}) %collective-permute-start.2) | collective-permute-done | bytes 131104 | tf_op jit(solution)/shard_map/ppermute | solution.py:32
  14.4 1.6 %collective-permute-start.3 = (f32[4,4,32,128]{3,2,1,0:T(8,128)S(1)}, f32[4,4,32,128]{3,2,1,0:T(8,128)S(1)}, u32[]{:S(2)}, u32[]{:S(2)}) collective-permute-start(f32[4,4,32,128]{3,2,1,0:T(8,128)S(1)} %bitcast.142), channel_id=1, source_target_pairs={{0,1},{1,0},{2,3},{3,2},{4,5},{5,4},{6,7},{7,6},{8,9},{9,8},{10,11... | collective-permute-start | bytes 786440 | tf_op jit(solution)/shard_map/ppermute | solution.py:32
  16.1 0.8 %collective-permute-done.4 = f32[2,4,32,128]{3,2,1,0:T(8,128)S(1)} collective-permute-done((f32[2,4,32,128]{3,2,1,0:T(8,128)S(1)}, f32[2,4,32,128]{3,2,1,0:T(8,128)S(1)}, u32[]{:S(2)}, u32[]{:S(2)}) %collective-permute-start.4) | collective-permute-done | bytes 131104 | tf_op jit(solution)/shard_map/ppermute | solution.py:32
  17.0 0.9 %collective-permute-start.5 = (f32[4,4,32,128]{3,2,1,0:T(8,128)S(1)}, f32[4,4,32,128]{3,2,1,0:T(8,128)S(1)}, u32[]{:S(2)}, u32[]{:S(2)}) collective-permute-start(f32[4,4,32,128]{3,2,1,0:T(8,128)S(1)} %bitcast.143), channel_id=1, source_target_pairs={{0,2},{1,3},{2,0},{3,1},{4,6},{5,7},{6,4},{7,5},{8,10},{9,11},{10,... | collective-permute-start | bytes 786440 | tf_op jit(solution)/shard_map/ppermute | solution.py:32
  17.9 4.5 %collective-permute-done.3 = f32[4,4,32,128]{3,2,1,0:T(8,128)S(1)} collective-permute-done((f32[4,4,32,128]{3,2,1,0:T(8,128)S(1)}, f32[4,4,32,128]{3,2,1,0:T(8,128)S(1)}, u32[]{:S(2)}, u32[]{:S(2)}) %collective-permute-start.3) | collective-permute-done | bytes 262176 | tf_op jit(solution)/shard_map/ppermute | solution.py:32
  22.3 1.6 %collective-permute-done.5 = f32[4,4,32,128]{3,2,1,0:T(8,128)S(1)} collective-permute-done((f32[4,4,32,128]{3,2,1,0:T(8,128)S(1)}, f32[4,4,32,128]{3,2,1,0:T(8,128)S(1)}, u32[]{:S(2)}, u32[]{:S(2)}) %collective-permute-start.5) | collective-permute-done | bytes 262176 | tf_op jit(solution)/shard_map/ppermute | solution.py:32
  23.9 0.1 select_bitcast_fusion.7
  24.2 0.0 copy-start.1
  24.2 1.0 %shard_map.38 = (f32[8,256,128]{2,1,0:T(8,128)S(1)}, f32[2,64,512]{2,1,0:T(8,128)S(1)}, f32[2,64,512]{2,1,0:T(8,128)S(1)}) custom-call(bf16[1024,512]{1,0:T(8,128)(2,1)S(1)} %get-tuple-element.43.ah_ref, bf16[1024,512]{1,0:T(8,128)(2,1)S(1)} %get-tuple-element.44.al_ref, f32[8,4,32,128]{3,2,1,0:T(8,128)S(1)} %bitcast.136, f32[8,4,32,128]{3,2,1,0:T(8,128)S(1)} %bitcast.135), custom_call_target="tpu_custom_call" | custom-call | flops 805306368 | bytes 4194304 | tf_op jit(solution)/shard_map/pallas_call | solution.py:252
  25.2 0.1 collective-permute-start.6
  25.3 1.5 %collective-permute-done.6 = f32[2,64,512]{2,1,0:T(8,128)S(1)} collective-permute-done((f32[2,64,512]{2,1,0:T(8,128)S(1)}, f32[2,64,512]{2,1,0:T(8,128)S(1)}, u32[]{:S(2)}, u32[]{:S(2)}) %collective-permute-start.6) | collective-permute-done | bytes 262176 | tf_op jit(solution)/shard_map/ppermute | solution.py:32
  26.9 1.1 %collective-permute-start.8 = (f32[64,512]{1,0:T(8,128)S(1)}, f32[64,512]{1,0:T(8,128)S(1)}, u32[]{:S(2)}, u32[]{:S(2)}) collective-permute-start(f32[64,512]{1,0:T(8,128)S(1)} %get-tuple-element.81), channel_id=1, source_target_pairs={{0,2},{1,10},{2,18},{3,26},{4,6},{5,14},{6,22},{7,30},{8,3},{9,11}... | collective-permute-start | bytes 393224 | tf_op jit(solution)/shard_map/ppermute | solution.py:232
  28.0 0.7 collective-permute-start.7
  28.7 0.0 copy-done.1
  28.7 1.0 %shard_map.39.ur_ref = bf16[1024,768]{1,0:T(8,128)(2,1)S(1)} custom-call(f32[256,256]{1,0:T(8,128)S(1)} %copy-done.1, f32[8,256,128]{2,1,0:T(8,128)S(1)} %get-tuple-element.66.y_ref), custom_call_target="tpu_custom_call" | custom-call | flops 402653184 | bytes 2097152 | tf_op jit(solution)/shard_map/pallas_call | solution.py:282
  29.8 4.3 %collective-permute-start.10 = (f32[1,64,512]{2,1,0:T(8,128)S(1)}, f32[1,64,512]{2,1,0:T(8,128)S(1)}, u32[]{:S(2)}, u32[]{:S(2)}) collective-permute-start(f32[1,64,512]{2,1,0:T(8,128)S(1)} %constant_dynamic-slice_fusion), channel_id=1, source_target_pairs={{0,16},{8,24},{16,0},{24,8},{1,17},{9,25},{17,1},{25,9},{2,18},{10... | collective-permute-start | bytes 393224 | tf_op jit(solution)/shard_map/ppermute | solution.py:32
  34.1 0.7 collective-permute-start.11
  34.8 0.0 collective-permute-done.8
  34.8 0.0 collective-permute-done.7
  34.8 3.4 %collective-permute-start.9 = (f32[1,32,512]{2,1,0:T(8,128)S(1)}, f32[1,32,512]{2,1,0:T(8,128)S(1)}, u32[]{:S(2)}, u32[]{:S(2)}) collective-permute-start(f32[1,32,512]{2,1,0:T(8,128)S(1)} %get-tuple-element.90), channel_id=1, source_target_pairs={{0,4},{1,5},{2,6},{3,7},{4,0},{5,1},{6,2},{7,3},{8,12},{9,13},{10,... | collective-permute-start | bytes 196616 | tf_op jit(solution)/shard_map/ppermute | solution.py:32
  38.3 0.1 collective-permute-start.16
  38.3 3.7 %collective-permute-done.10 = f32[1,64,512]{2,1,0:T(8,128)S(1)} collective-permute-done((f32[1,64,512]{2,1,0:T(8,128)S(1)}, f32[1,64,512]{2,1,0:T(8,128)S(1)}, u32[]{:S(2)}, u32[]{:S(2)}) %collective-permute-start.10) | collective-permute-done | bytes 131104 | tf_op jit(solution)/shard_map/ppermute | solution.py:32
  42.0 0.0 collective-permute-done.11
  42.1 0.0 collective-permute-done.9
  42.1 4.2 %collective-permute-start.14 = (f32[2,32,512]{2,1,0:T(8,128)S(1)}, f32[2,32,512]{2,1,0:T(8,128)S(1)}, u32[]{:S(2)}, u32[]{:S(2)}) collective-permute-start(f32[2,32,512]{2,1,0:T(8,128)S(1)} %maximum_bitcast_fusion.3.first_ref), channel_id=1, source_target_pairs={{0,2},{1,3},{2,0},{3,1},{4,6},{5,7},{6,4},{7,5},{8,10},{9,11},{10,... | collective-permute-start | bytes 393224 | tf_op jit(solution)/shard_map/ppermute | solution.py:32
  46.3 0.0 collective-permute-done.16
  46.3 1.4 %collective-permute-start.17 = (f32[2,32,512]{2,1,0:T(8,128)S(1)}, f32[2,32,512]{2,1,0:T(8,128)S(1)}, u32[]{:S(2)}, u32[]{:S(2)}) collective-permute-start(f32[2,32,512]{2,1,0:T(8,128)S(1)} %maximum_bitcast_fusion.4.second_ref), channel_id=1, source_target_pairs={{0,1},{1,0},{2,3},{3,2},{4,5},{5,4},{6,7},{7,6},{8,9},{9,8},{10,11... | collective-permute-start | bytes 393224 | tf_op jit(solution)/shard_map/ppermute | solution.py:32
  47.7 0.5 collective-permute-start.12
  48.2 2.4 %collective-permute-done.14 = f32[2,32,512]{2,1,0:T(8,128)S(1)} collective-permute-done((f32[2,32,512]{2,1,0:T(8,128)S(1)}, f32[2,32,512]{2,1,0:T(8,128)S(1)}, u32[]{:S(2)}, u32[]{:S(2)}) %collective-permute-start.14) | collective-permute-done | bytes 131104 | tf_op jit(solution)/shard_map/ppermute | solution.py:32
  50.7 0.7 shard_map.42
  51.3 0.1 collective-permute-start.19
  51.4 0.1 collective-permute-start.15
  51.5 0.8 %collective-permute-done.17 = f32[2,32,512]{2,1,0:T(8,128)S(1)} collective-permute-done((f32[2,32,512]{2,1,0:T(8,128)S(1)}, f32[2,32,512]{2,1,0:T(8,128)S(1)}, u32[]{:S(2)}, u32[]{:S(2)}) %collective-permute-start.17) | collective-permute-done | bytes 131104 | tf_op jit(solution)/shard_map/ppermute | solution.py:32
  52.4 1.1 %collective-permute-start.18 = (f32[4,32,512]{2,1,0:T(8,128)S(1)}, f32[4,32,512]{2,1,0:T(8,128)S(1)}, u32[]{:S(2)}, u32[]{:S(2)}) collective-permute-start(f32[4,32,512]{2,1,0:T(8,128)S(1)} %bitcast.137), channel_id=1, source_target_pairs={{0,2},{1,3},{2,0},{3,1},{4,6},{5,7},{6,4},{7,5},{8,10},{9,11},{10,... | collective-permute-start | bytes 786440 | tf_op jit(solution)/shard_map/ppermute | solution.py:32
  53.5 0.0 collective-permute-done.19
  53.5 0.8 %collective-permute-start.20 = (f32[32,512]{1,0:T(8,128)S(1)}, f32[32,512]{1,0:T(8,128)S(1)}, u32[]{:S(2)}, u32[]{:S(2)}) collective-permute-start(f32[32,512]{1,0:T(8,128)S(1)} %add.18), channel_id=1, source_target_pairs={{0,16},{8,24},{16,0},{24,8},{1,17},{9,25},{17,1},{25,9},{2,18},{10... | collective-permute-start | bytes 196616 | tf_op jit(solution)/shard_map/ppermute | solution.py:32
  54.3 1.9 %collective-permute-done.12 = f32[1,4,32,512]{3,2,1,0:T(8,128)S(1)} collective-permute-done((f32[1,4,32,512]{3,2,1,0:T(8,128)S(1)}, f32[1,4,32,512]{3,2,1,0:T(8,128)S(1)}, u32[]{:S(2)}, u32[]{:S(2)}) %collective-permute-start.12) | collective-permute-done | bytes 262176 | tf_op jit(solution)/shard_map/ppermute | solution.py:32
  56.3 0.1 collective-permute-start.13
  56.4 1.4 %collective-permute-done.20 = f32[32,512]{1,0:T(8,128)S(1)} collective-permute-done((f32[32,512]{1,0:T(8,128)S(1)}, f32[32,512]{1,0:T(8,128)S(1)}, u32[]{:S(2)}, u32[]{:S(2)}) %collective-permute-start.20) | collective-permute-done | bytes 65568 | tf_op jit(solution)/shard_map/ppermute | solution.py:32
  57.8 1.7 %collective-permute-start.23 = (f32[1,32,512]{2,1,0:T(8,128)S(1)}, f32[1,32,512]{2,1,0:T(8,128)S(1)}, u32[]{:S(2)}, u32[]{:S(2)}) collective-permute-start(f32[1,32,512]{2,1,0:T(8,128)S(1)} %add_bitcast_fusion.refs_0_), channel_id=1, source_target_pairs={{0,3},{1,2},{2,1},{3,0},{4,7},{5,6},{6,5},{7,4},{8,11},{9,10},{10,... | collective-permute-start | bytes 196616 | tf_op jit(solution)/shard_map/ppermute | solution.py:32
  59.6 1.3 %collective-permute-start.22 = (f32[1,32,512]{2,1,0:T(8,128)S(1)}, f32[1,32,512]{2,1,0:T(8,128)S(1)}, u32[]{:S(2)}, u32[]{:S(2)}) collective-permute-start(f32[1,32,512]{2,1,0:T(8,128)S(1)} %add_bitcast_fusion.refs_0_), channel_id=1, source_target_pairs={{0,2},{1,3},{2,0},{3,1},{4,6},{5,7},{6,4},{7,5},{8,10},{9,11},{10,... | collective-permute-start | bytes 196616 | tf_op jit(solution)/shard_map/ppermute | solution.py:32
  60.8 0.0 collective-permute-done.15
  60.9 0.6 collective-permute-start.21
  61.5 0.0 collective-permute-done.13
  61.5 0.1 select_bitcast_fusion.1
  61.6 0.1 pad_maximum_fusion
  61.7 0.4 shard_map.40
  62.2 0.0 collective-permute-done.18.came_ref
  62.2 1.1 %shard_map.41.rest_ref = f32[1024,512]{1,0:T(8,128)S(1)} custom-call(f32[1024,512]{1,0:T(8,128)S(1)} %get-tuple-element.36.a_ref, bf16[768,512]{1,0:T(8,128)(2,1)S(1)} %get-tuple-element.61.uc_ref, f32[8,32,512]{2,1,0:T(8,128)S(1)} %bitcast.133, f32[4,32,512]{2,1,0:T(8,128)S(1)} %bitcast.138, f32[4,32,512]{2,1,0:T(8,128)S(1)} %collective-permute-done.18.came_ref), custom_call_target="tpu_custom_call" | custom-call | flops 805306368 | bytes 4194304 | tf_op jit(solution)/shard_map/pallas_call | solution.py:334
  63.3 0.4 collective-permute-done.23.refs_3_
  63.6 0.4 collective-permute-done.22.refs_2_
  64.0 1.1 %collective-permute-done.21.refs_1_ = f32[1,32,512]{2,1,0:T(8,128)S(1)} collective-permute-done((f32[1,32,512]{2,1,0:T(8,128)S(1)}, f32[1,32,512]{2,1,0:T(8,128)S(1)}, u32[]{:S(2)}, u32[]{:S(2)}) %collective-permute-start.21) | collective-permute-done | bytes 65568 | tf_op jit(solution)/shard_map/ppermute | solution.py:32
  65.1 2.2 %shard_map.43 = f32[4096,128]{1,0:T(8,128)} custom-call(f32[1024,512]{1,0:T(8,128)S(1)} %shard_map.41.rest_ref, bf16[1024,768]{1,0:T(8,128)(2,1)S(1)} %shard_map.39.ur_ref, bf16[768,512]{1,0:T(8,128)(2,1)S(1)} %get-tuple-element.61.uc_ref, f32[256,512]{1,0:T(8,128)S(1)} %get-tuple-element.65.zc_ref, f32[1,32,512]{2,1,0:T(8,128)S(1)} %add_bitcast_fusion.refs_0_, ...), custom_call_target="tpu_custom_call" | custom-call | flops 805306368 | bytes 4194304 | tf_op jit(solution)/shard_map/pallas_call | solution.py:345
  (32 shorter events, 0.7 us)
Async XLA Ops:
  0.9 7.8 %collective-permute-start.1 = (f32[1,4,32,128]{3,2,1,0:T(8,128)S(1)}, f32[1,4,32,128]{3,2,1,0:T(8,128)S(1)}, u32[]{:S(2)}, u32[]{:S(2)}) collective-permute-start(f32[1,4,32,128]{3,2,1,0:T(8,128)S(1)} %get-tuple-element.97), channel_id=1, source_target_pairs={{0,4},{1,5},{2,6},{3,7},{4,0},{5,1},{6,2},{7,3},{8,12},{9,13},{10,... | collective-permute-start | bytes 196616 | tf_op jit(solution)/shard_map/ppermute | solution.py:32
  5.0 6.5 %collective-permute-start = (f32[1,4,32,128]{3,2,1,0:T(8,128)S(1)}, f32[1,4,32,128]{3,2,1,0:T(8,128)S(1)}, u32[]{:S(2)}, u32[]{:S(2)}) collective-permute-start(f32[1,4,32,128]{3,2,1,0:T(8,128)S(1)} %get-tuple-element.98), channel_id=1, source_target_pairs={{0,4},{1,5},{2,6},{3,7},{4,0},{5,1},{6,2},{7,3},{8,12},{9,13},{10,... | collective-permute-start | bytes 196616 | tf_op jit(solution)/shard_map/ppermute | solution.py:32
  5.1 1.6 %copy-start = (f32[8,1,128,4,1,128]{5,4,3,2,1,0:T(1,128)S(1)}, f32[8,1,128,4,1,128]{5,4,3,2,1,0:T(1,128)}, u32[]{:S(2)}) copy-start(f32[8,1,128,4,1,128]{5,4,3,2,1,0:T(1,128)} %param.3) | copy-start | bytes 6291460
  8.7 5.7 %collective-permute-start.2 = (f32[2,4,32,128]{3,2,1,0:T(8,128)S(1)}, f32[2,4,32,128]{3,2,1,0:T(8,128)S(1)}, u32[]{:S(2)}, u32[]{:S(2)}) collective-permute-start(f32[2,4,32,128]{3,2,1,0:T(8,128)S(1)} %maximum_bitcast_fusion.1), channel_id=1, source_target_pairs={{0,2},{1,3},{2,0},{3,1},{4,6},{5,7},{6,4},{7,5},{8,10},{9,11},{10,... | collective-permute-start | bytes 393224 | tf_op jit(solution)/shard_map/ppermute | solution.py:32
  11.5 5.4 %collective-permute-start.4 = (f32[2,4,32,128]{3,2,1,0:T(8,128)S(1)}, f32[2,4,32,128]{3,2,1,0:T(8,128)S(1)}, u32[]{:S(2)}, u32[]{:S(2)}) collective-permute-start(f32[2,4,32,128]{3,2,1,0:T(8,128)S(1)} %maximum_bitcast_fusion.2), channel_id=1, source_target_pairs={{0,1},{1,0},{2,3},{3,2},{4,5},{5,4},{6,7},{7,6},{8,9},{9,8},{10,11... | collective-permute-start | bytes 393224 | tf_op jit(solution)/shard_map/ppermute | solution.py:32
  14.4 7.9 %collective-permute-start.3 = (f32[4,4,32,128]{3,2,1,0:T(8,128)S(1)}, f32[4,4,32,128]{3,2,1,0:T(8,128)S(1)}, u32[]{:S(2)}, u32[]{:S(2)}) collective-permute-start(f32[4,4,32,128]{3,2,1,0:T(8,128)S(1)} %bitcast.142), channel_id=1, source_target_pairs={{0,1},{1,0},{2,3},{3,2},{4,5},{5,4},{6,7},{7,6},{8,9},{9,8},{10,11... | collective-permute-start | bytes 786440 | tf_op jit(solution)/shard_map/ppermute | solution.py:32
  17.0 7.0 %collective-permute-start.5 = (f32[4,4,32,128]{3,2,1,0:T(8,128)S(1)}, f32[4,4,32,128]{3,2,1,0:T(8,128)S(1)}, u32[]{:S(2)}, u32[]{:S(2)}) collective-permute-start(f32[4,4,32,128]{3,2,1,0:T(8,128)S(1)} %bitcast.143), channel_id=1, source_target_pairs={{0,2},{1,3},{2,0},{3,1},{4,6},{5,7},{6,4},{7,5},{8,10},{9,11},{10,... | collective-permute-start | bytes 786440 | tf_op jit(solution)/shard_map/ppermute | solution.py:32
  24.2 4.6 %copy-start.1 = (f32[256,256]{1,0:T(8,128)S(1)}, f32[256,256]{1,0:T(8,128)}, u32[]{:S(2)}) copy-start(f32[256,256]{1,0:T(8,128)} %t_ref.3) | copy-start | bytes 786436
  25.2 1.6 %collective-permute-start.6 = (f32[2,64,512]{2,1,0:T(8,128)S(1)}, f32[2,64,512]{2,1,0:T(8,128)S(1)}, u32[]{:S(2)}, u32[]{:S(2)}) collective-permute-start(f32[2,64,512]{2,1,0:T(8,128)S(1)} %get-tuple-element.49), channel_id=1, source_target_pairs={{0,8},{8,0},{16,24},{24,16},{1,9},{9,1},{17,25},{25,17},{2,10},{10... | collective-permute-start | bytes 786440 | tf_op jit(solution)/shard_map/ppermute | solution.py:32
  26.9 7.9 %collective-permute-start.8 = (f32[64,512]{1,0:T(8,128)S(1)}, f32[64,512]{1,0:T(8,128)S(1)}, u32[]{:S(2)}, u32[]{:S(2)}) collective-permute-start(f32[64,512]{1,0:T(8,128)S(1)} %get-tuple-element.81), channel_id=1, source_target_pairs={{0,2},{1,10},{2,18},{3,26},{4,6},{5,14},{6,22},{7,30},{8,3},{9,11}... | collective-permute-start | bytes 393224 | tf_op jit(solution)/shard_map/ppermute | solution.py:232
  28.0 6.7 %collective-permute-start.7 = (f32[64,512]{1,0:T(8,128)S(1)}, f32[64,512]{1,0:T(8,128)S(1)}, u32[]{:S(2)}, u32[]{:S(2)}) collective-permute-start(f32[64,512]{1,0:T(8,128)S(1)} %get-tuple-element.82), channel_id=1, source_target_pairs={{0,0},{1,8},{2,16},{3,24},{4,4},{5,12},{6,20},{7,28},{8,1},{9,9},{... | collective-permute-start | bytes 393224 | tf_op jit(solution)/shard_map/ppermute | solution.py:232
  29.8 12.2 %collective-permute-start.10 = (f32[1,64,512]{2,1,0:T(8,128)S(1)}, f32[1,64,512]{2,1,0:T(8,128)S(1)}, u32[]{:S(2)}, u32[]{:S(2)}) collective-permute-start(f32[1,64,512]{2,1,0:T(8,128)S(1)} %constant_dynamic-slice_fusion), channel_id=1, source_target_pairs={{0,16},{8,24},{16,0},{24,8},{1,17},{9,25},{17,1},{25,9},{2,18},{10... | collective-permute-start | bytes 393224 | tf_op jit(solution)/shard_map/ppermute | solution.py:32
  34.1 7.9 %collective-permute-start.11 = (f32[64,512]{1,0:T(8,128)S(1)}, f32[64,512]{1,0:T(8,128)S(1)}, u32[]{:S(2)}, u32[]{:S(2)}) collective-permute-start(f32[64,512]{1,0:T(8,128)S(1)} %copy_bitcast_fusion), channel_id=1, source_target_pairs={{0,0},{1,8},{2,16},{3,24},{4,4},{5,12},{6,20},{7,28},{8,1},{9,9},{... | collective-permute-start | bytes 393224 | tf_op jit(solution)/shard_map/ppermute | solution.py:232
  34.8 7.2 %collective-permute-start.9 = (f32[1,32,512]{2,1,0:T(8,128)S(1)}, f32[1,32,512]{2,1,0:T(8,128)S(1)}, u32[]{:S(2)}, u32[]{:S(2)}) collective-permute-start(f32[1,32,512]{2,1,0:T(8,128)S(1)} %get-tuple-element.90), channel_id=1, source_target_pairs={{0,4},{1,5},{2,6},{3,7},{4,0},{5,1},{6,2},{7,3},{8,12},{9,13},{10,... | collective-permute-start | bytes 196616 | tf_op jit(solution)/shard_map/ppermute | solution.py:32
  38.3 8.0 %collective-permute-start.16 = (f32[1,32,512]{2,1,0:T(8,128)S(1)}, f32[1,32,512]{2,1,0:T(8,128)S(1)}, u32[]{:S(2)}, u32[]{:S(2)}) collective-permute-start(f32[1,32,512]{2,1,0:T(8,128)S(1)} %get-tuple-element.89), channel_id=1, source_target_pairs={{0,4},{1,5},{2,6},{3,7},{4,0},{5,1},{6,2},{7,3},{8,12},{9,13},{10,... | collective-permute-start | bytes 196616 | tf_op jit(solution)/shard_map/ppermute | solution.py:32
  42.1 8.5 %collective-permute-start.14 = (f32[2,32,512]{2,1,0:T(8,128)S(1)}, f32[2,32,512]{2,1,0:T(8,128)S(1)}, u32[]{:S(2)}, u32[]{:S(2)}) collective-permute-start(f32[2,32,512]{2,1,0:T(8,128)S(1)} %maximum_bitcast_fusion.3.first_ref), channel_id=1, source_target_pairs={{0,2},{1,3},{2,0},{3,1},{4,6},{5,7},{6,4},{7,5},{8,10},{9,11},{10,... | collective-permute-start | bytes 393224 | tf_op jit(solution)/shard_map/ppermute | solution.py:32
  46.3 6.0 %collective-permute-start.17 = (f32[2,32,512]{2,1,0:T(8,128)S(1)}, f32[2,32,512]{2,1,0:T(8,128)S(1)}, u32[]{:S(2)}, u32[]{:S(2)}) collective-permute-start(f32[2,32,512]{2,1,0:T(8,128)S(1)} %maximum_bitcast_fusion.4.second_ref), channel_id=1, source_target_pairs={{0,1},{1,0},{2,3},{3,2},{4,5},{5,4},{6,7},{7,6},{8,9},{9,8},{10,11... | collective-permute-start | bytes 393224 | tf_op jit(solution)/shard_map/ppermute | solution.py:32
  47.7 8.5 %collective-permute-start.12 = (f32[1,4,32,512]{3,2,1,0:T(8,128)S(1)}, f32[1,4,32,512]{3,2,1,0:T(8,128)S(1)}, u32[]{:S(2)}, u32[]{:S(2)}) collective-permute-start(f32[1,4,32,512]{3,2,1,0:T(8,128)S(1)} %bitcast.139), channel_id=1, source_target_pairs={{0,16},{8,24},{16,0},{24,8},{1,17},{9,25},{17,1},{25,9},{2,18},{10... | collective-permute-start | bytes 786440 | tf_op jit(solution)/shard_map/ppermute | solution.py:32
  51.3 2.2 %collective-permute-start.19 = (f32[32,512]{1,0:T(8,128)S(1)}, f32[32,512]{1,0:T(8,128)S(1)}, u32[]{:S(2)}, u32[]{:S(2)}) collective-permute-start(f32[32,512]{1,0:T(8,128)S(1)} %shard_map.42), channel_id=1, source_target_pairs={{0,8},{8,0},{16,24},{24,16},{1,9},{9,1},{17,25},{25,17},{2,10},{10... | collective-permute-start | bytes 196616 | tf_op jit(solution)/shard_map/ppermute | solution.py:32
  51.4 9.5 %collective-permute-start.15 = (f32[4,32,512]{2,1,0:T(8,128)S(1)}, f32[4,32,512]{2,1,0:T(8,128)S(1)}, u32[]{:S(2)}, u32[]{:S(2)}) collective-permute-start(f32[4,32,512]{2,1,0:T(8,128)S(1)} %bitcast.140), channel_id=1, source_target_pairs={{0,1},{1,0},{2,3},{3,2},{4,5},{5,4},{6,7},{7,6},{8,9},{9,8},{10,11... | collective-permute-start | bytes 786440 | tf_op jit(solution)/shard_map/ppermute | solution.py:32
  52.4 9.8 %collective-permute-start.18 = (f32[4,32,512]{2,1,0:T(8,128)S(1)}, f32[4,32,512]{2,1,0:T(8,128)S(1)}, u32[]{:S(2)}, u32[]{:S(2)}) collective-permute-start(f32[4,32,512]{2,1,0:T(8,128)S(1)} %bitcast.137), channel_id=1, source_target_pairs={{0,2},{1,3},{2,0},{3,1},{4,6},{5,7},{6,4},{7,5},{8,10},{9,11},{10,... | collective-permute-start | bytes 786440 | tf_op jit(solution)/shard_map/ppermute | solution.py:32
  53.5 4.3 %collective-permute-start.20 = (f32[32,512]{1,0:T(8,128)S(1)}, f32[32,512]{1,0:T(8,128)S(1)}, u32[]{:S(2)}, u32[]{:S(2)}) collective-permute-start(f32[32,512]{1,0:T(8,128)S(1)} %add.18), channel_id=1, source_target_pairs={{0,16},{8,24},{16,0},{24,8},{1,17},{9,25},{17,1},{25,9},{2,18},{10... | collective-permute-start | bytes 196616 | tf_op jit(solution)/shard_map/ppermute | solution.py:32
  56.3 5.2 %collective-permute-start.13 = (f32[2,4,32,512]{3,2,1,0:T(8,128)S(1)}, f32[2,4,32,512]{3,2,1,0:T(8,128)S(1)}, u32[]{:S(2)}, u32[]{:S(2)}) collective-permute-start(f32[2,4,32,512]{3,2,1,0:T(8,128)S(1)} %maximum_bitcast_fusion), channel_id=1, source_target_pairs={{0,8},{8,0},{16,24},{24,16},{1,9},{9,1},{17,25},{25,17},{2,10},{10... | collective-permute-start | bytes 1572872 | tf_op jit(solution)/shard_map/ppermute | solution.py:32
  57.8 5.8 %collective-permute-start.23 = (f32[1,32,512]{2,1,0:T(8,128)S(1)}, f32[1,32,512]{2,1,0:T(8,128)S(1)}, u32[]{:S(2)}, u32[]{:S(2)}) collective-permute-start(f32[1,32,512]{2,1,0:T(8,128)S(1)} %add_bitcast_fusion.refs_0_), channel_id=1, source_target_pairs={{0,3},{1,2},{2,1},{3,0},{4,7},{5,6},{6,5},{7,4},{8,11},{9,10},{10,... | collective-permute-start | bytes 196616 | tf_op jit(solution)/shard_map/ppermute | solution.py:32
  59.6 4.4 %collective-permute-start.22 = (f32[1,32,512]{2,1,0:T(8,128)S(1)}, f32[1,32,512]{2,1,0:T(8,128)S(1)}, u32[]{:S(2)}, u32[]{:S(2)}) collective-permute-start(f32[1,32,512]{2,1,0:T(8,128)S(1)} %add_bitcast_fusion.refs_0_), channel_id=1, source_target_pairs={{0,2},{1,3},{2,0},{3,1},{4,6},{5,7},{6,4},{7,5},{8,10},{9,11},{10,... | collective-permute-start | bytes 196616 | tf_op jit(solution)/shard_map/ppermute | solution.py:32
  60.9 4.3 %collective-permute-start.21 = (f32[1,32,512]{2,1,0:T(8,128)S(1)}, f32[1,32,512]{2,1,0:T(8,128)S(1)}, u32[]{:S(2)}, u32[]{:S(2)}) collective-permute-start(f32[1,32,512]{2,1,0:T(8,128)S(1)} %add_bitcast_fusion.refs_0_), channel_id=1, source_target_pairs={{0,1},{1,0},{2,3},{3,2},{4,5},{5,4},{6,7},{7,6},{8,9},{9,8},{10,11... | collective-permute-start | bytes 196616 | tf_op jit(solution)/shard_map/ppermute | solution.py:32

commit v3 on v2

--- a/solution.py
+++ b/solution.py
@@ -65,7 +65,8 @@
     return [swap(values, axis, mask) for mask in (1, 2, 3)]
 
 
-def split_block_kernel(col_tiles, tile, a_ref, high_ref, low_ref, copy_ref):
+def split_block_kernel(col_tiles, tile, a_ref, y_ref, high_ref, low_ref, copy_ref, y_copy_ref):
+    y_copy_ref[...] = y_ref[...]
     rows = high_ref.shape[0]
     for b in range(col_tiles):
         cols = slice(b * tile, (b + 1) * tile)
@@ -234,19 +235,20 @@
     inner_upper = [mask // 4 for mask in rest[:-2]]
     far, close = rest[-2:]
     orders = (masks, masks[:-2] + [close, far])
-    a_high, a_low, a_full = pl.pallas_call(
+    a_high, a_low, a_full, y = pl.pallas_call(
         functools.partial(split_block_kernel, col_tiles, tile),
-        out_shape=[shape(rows, cols, dtype=BF16)] * 2 + [shape(rows, cols)],
-        in_specs=[whole],
-        out_specs=[whole] * 3,
+        out_shape=[shape(rows, cols, dtype=BF16)] * 2 + [shape(rows, cols), shape(*mine.shape)],
+        in_specs=[whole] * 2,
+        out_specs=[whole] * 4,
         compiler_params=VMEM,
         cost_estimate=pl.CostEstimate(flops=rows * cols * 4, bytes_accessed=rows * cols * 8, transcendentals=0),
-    )(block)
-    first, second = lax.optimization_barrier(mine[None, :half]), lax.optimization_barrier(mine[None, half:])
-    for at, (mask, other) in enumerate(zip(*orders)):
+    )(block, mine)
+    y = y[None]
+    for at, mask in enumerate(lead):
+        y = join(y, swap(mine[None] if at == 0 else y, "pcol", mask), col[mask])
+    first, second = lax.optimization_barrier(y[:, :half]), lax.optimization_barrier(y[:, half:])
+    for mask, other in zip(orders[0][len(lead) :], orders[1][len(lead) :]):
         first_came, second_came = swap(first, "pcol", mask), swap(second, "pcol", other)
-        if at == 0:
-            second_came, a_high, a_low = lax.optimization_barrier((second_came, a_high, a_low))
         first, second = join(first, first_came, col[mask]), join(second, second_came, col[other])
 
     y_rows, keep, send = pl.pallas_call(

time: 67.5 us -> 67.7 us (level)
  waiting for transfers between devices: 23.5 us -> 25.1 us
  starting transfers between devices: 32.7 us -> 31.3 us
    ppermute x21 -> x20, waiting for transfers between devices: 23.5 us -> 25.1 us  [swap(): return lax.ppermute(values, axis, [(i, i ^ mask) for i in range(n)])]
    ppermute x21 -> x20, starting transfers between devices: 30.2 us -> 28.9 us  [swap(): return lax.ppermute(values, axis, [(i, i ^ mask) for i in range(n)])]
    unnamed x4 -> x6, local copies, waits for them, and re-layouts: 1.6 us -> 2.5 us
    broadcast_in_dim x1 -> x0, local copies, waits for them, and re-layouts: 0.88 us -> none  [per_device(): mine[None, :half]]
  transfers between devices with their start and end apart: 24 -> 23, of which waited for: 15 -> 15; matrix products, arithmetic and copies ran while one was open for 1% -> 1% of each run, Pallas kernels for 6% -> 6%
where the time goes in v3:
time: 67.7 us; the launch traced here: 67.5 us
  starting transfers between devices  31.3 us (46%)
  waiting for transfers between devices  25.1 us (37%)
  Pallas kernels  7.24 us (11%)
  local copies, waits for them, and re-layouts  2.6 us (4%)
  other arithmetic  0.93 us (1%)
    ppermute x20, starting transfers between devices, swap(): return lax.ppermute(values, axis, [(i, i ^ mask) for i in range(n)])  28.9 us
    ppermute x20, waiting for transfers between devices, swap(): return lax.ppermute(values, axis, [(i, i ^ mask) for i in range(n)])  25.1 us
    unnamed x6, local copies, waits for them, and re-layouts  2.5 us
    ppermute x3, starting transfers between devices, turn(): return lax.ppermute(values, BOTH, perm)  2.41 us
    pallas_call x1, Pallas kernels, per_device(): pl.pallas_call(functools.partial(update_kernel, inner_upper), out_shape=s...  2.15 us
  transfers between devices with their start and end apart: 23, of which 15 were waited for; matrix products, arithmetic and copies ran while one was open for 1% of the time, Pallas kernels for 6%

profile of v3, /device:TPU:0, one launch (start us, length us, event | category | flops | bytes accessed | tf_op | source)
XLA Modules:
  0.0 67.5 jit_solution(10600988103644421862)
XLA Ops:
  0.0 4.0 %collective-permute-start = (f32[1,8,32,128]{3,2,1,0:T(8,128)}, f32[1,8,32,128]{3,2,1,0:T(8,128)S(1)}, u32[]{:S(2)}, u32[]{:S(2)}) collective-permute-start(f32[1,8,32,128]{3,2,1,0:T(8,128)} %bitcast.129), channel_id=1, source_target_pairs={{0,4},{1,5},{2,6},{3,7},{4,0},{5,1},{6,2},{7,3},{8,12},{9,13},{10,... | collective-permute-start | bytes 393224 | tf_op jit(solution)/shard_map/ppermute | solution.py:32
  4.0 0.0 copy-start
  4.0 1.6 %copy-done = f32[8,1,128,4,1,128]{5,4,3,2,1,0:T(1,128)S(1)} copy-done((f32[8,1,128,4,1,128]{5,4,3,2,1,0:T(1,128)S(1)}, f32[8,1,128,4,1,128]{5,4,3,2,1,0:T(1,128)}, u32[]{:S(2)}) %copy-start) | copy-done | bytes 2097176
  5.6 0.0 copy-start.2
  5.6 0.9 %copy-done.2 = f32[8,1,128,32]{2,3,1,0:T(8,128)S(1)} copy-done((f32[8,1,128,32]{2,3,1,0:T(8,128)S(1)}, f32[8,1,128,32]{2,3,1,0:T(8,128)}, u32[]{:S(2)}) %copy-start.2) | copy-done | bytes 131096
  6.5 0.8 %shard_map.37 = (bf16[1024,512]{1,0:T(8,128)(2,1)S(1)}, bf16[1024,512]{1,0:T(8,128)(2,1)S(1)}, f32[1024,512]{1,0:T(8,128)S(1)}, f32[8,32,128]{2,1,0:T(8,128)S(1)}) custom-call(f32[4096,128]{1,0:T(8,128)S(1)} %bitcast.124, f32[8,32,128]{2,1,0:T(8,128)S(1)} %bitcast.130), custom_call_target="tpu_custom_call" | custom-call | flops 2097152 | bytes 4194304 | tf_op jit(solution)/shard_map/pallas_call | solution.py:238
  7.3 3.2 %collective-permute-done = f32[1,8,32,128]{3,2,1,0:T(8,128)S(1)} collective-permute-done((f32[1,8,32,128]{3,2,1,0:T(8,128)}, f32[1,8,32,128]{3,2,1,0:T(8,128)S(1)}, u32[]{:S(2)}, u32[]{:S(2)}) %collective-permute-start) | collective-permute-done | bytes 131104 | tf_op jit(solution)/shard_map/ppermute | solution.py:32
  10.6 1.6 %collective-permute-start.3 = (f32[2,4,32,128]{3,2,1,0:T(8,128)S(1)}, f32[2,4,32,128]{3,2,1,0:T(8,128)S(1)}, u32[]{:S(2)}, u32[]{:S(2)}) collective-permute-start(f32[2,4,32,128]{3,2,1,0:T(8,128)S(1)} %get-tuple-element.81), channel_id=1, source_target_pairs={{0,1},{1,0},{2,3},{3,2},{4,5},{5,4},{6,7},{7,6},{8,9},{9,8},{10,11... | collective-permute-start | bytes 393224 | tf_op jit(solution)/shard_map/ppermute | solution.py:32
  12.2 0.8 %collective-permute-start.1 = (f32[2,4,32,128]{3,2,1,0:T(8,128)S(1)}, f32[2,4,32,128]{3,2,1,0:T(8,128)S(1)}, u32[]{:S(2)}, u32[]{:S(2)}) collective-permute-start(f32[2,4,32,128]{3,2,1,0:T(8,128)S(1)} %get-tuple-element.82), channel_id=1, source_target_pairs={{0,2},{1,3},{2,0},{3,1},{4,6},{5,7},{6,4},{7,5},{8,10},{9,11},{10,... | collective-permute-start | bytes 393224 | tf_op jit(solution)/shard_map/ppermute | solution.py:32
  13.0 2.6 %collective-permute-done.3 = f32[2,4,32,128]{3,2,1,0:T(8,128)S(1)} collective-permute-done((f32[2,4,32,128]{3,2,1,0:T(8,128)S(1)}, f32[2,4,32,128]{3,2,1,0:T(8,128)S(1)}, u32[]{:S(2)}, u32[]{:S(2)}) %collective-permute-start.3) | collective-permute-done | bytes 131104 | tf_op jit(solution)/shard_map/ppermute | solution.py:32
  15.7 1.3 %collective-permute-start.4 = (f32[4,4,32,128]{3,2,1,0:T(8,128)S(1)}, f32[4,4,32,128]{3,2,1,0:T(8,128)S(1)}, u32[]{:S(2)}, u32[]{:S(2)}) collective-permute-start(f32[4,4,32,128]{3,2,1,0:T(8,128)S(1)} %bitcast.134), channel_id=1, source_target_pairs={{0,2},{1,3},{2,0},{3,1},{4,6},{5,7},{6,4},{7,5},{8,10},{9,11},{10,... | collective-permute-start | bytes 786440 | tf_op jit(solution)/shard_map/ppermute | solution.py:32
  17.1 0.2 collective-permute-done.1
  17.3 1.3 %collective-permute-start.2 = (f32[4,4,32,128]{3,2,1,0:T(8,128)S(1)}, f32[4,4,32,128]{3,2,1,0:T(8,128)S(1)}, u32[]{:S(2)}, u32[]{:S(2)}) collective-permute-start(f32[4,4,32,128]{3,2,1,0:T(8,128)S(1)} %bitcast.135), channel_id=1, source_target_pairs={{0,1},{1,0},{2,3},{3,2},{4,5},{5,4},{6,7},{7,6},{8,9},{9,8},{10,11... | collective-permute-start | bytes 786440 | tf_op jit(solution)/shard_map/ppermute | solution.py:32
  18.7 4.2 %collective-permute-done.4 = f32[4,4,32,128]{3,2,1,0:T(8,128)S(1)} collective-permute-done((f32[4,4,32,128]{3,2,1,0:T(8,128)S(1)}, f32[4,4,32,128]{3,2,1,0:T(8,128)S(1)}, u32[]{:S(2)}, u32[]{:S(2)}) %collective-permute-start.4) | collective-permute-done | bytes 262176 | tf_op jit(solution)/shard_map/ppermute | solution.py:32
  22.8 1.5 %collective-permute-done.2 = f32[4,4,32,128]{3,2,1,0:T(8,128)S(1)} collective-permute-done((f32[4,4,32,128]{3,2,1,0:T(8,128)S(1)}, f32[4,4,32,128]{3,2,1,0:T(8,128)S(1)}, u32[]{:S(2)}, u32[]{:S(2)}) %collective-permute-start.2) | collective-permute-done | bytes 262176 | tf_op jit(solution)/shard_map/ppermute | solution.py:32
  24.3 0.1 select_bitcast_fusion.7
  24.5 0.0 copy-start.1
  24.5 1.1 %shard_map.38 = (f32[8,256,128]{2,1,0:T(8,128)S(1)}, f32[2,64,512]{2,1,0:T(8,128)S(1)}, f32[2,64,512]{2,1,0:T(8,128)S(1)}) custom-call(bf16[1024,512]{1,0:T(8,128)(2,1)S(1)} %get-tuple-element.39.ah_ref, bf16[1024,512]{1,0:T(8,128)(2,1)S(1)} %get-tuple-element.40.al_ref, f32[8,4,32,128]{3,2,1,0:T(8,128)S(1)} %bitcast.126, f32[8,4,32,128]{3,2,1,0:T(8,128)S(1)} %bitcast.125), custom_call_target="tpu_custom_call" | custom-call | flops 805306368 | bytes 4194304 | tf_op jit(solution)/shard_map/pallas_call | solution.py:254
  25.6 0.1 collective-permute-start.5
  25.7 1.5 %collective-permute-done.5 = f32[2,64,512]{2,1,0:T(8,128)S(1)} collective-permute-done((f32[2,64,512]{2,1,0:T(8,128)S(1)}, f32[2,64,512]{2,1,0:T(8,128)S(1)}, u32[]{:S(2)}, u32[]{:S(2)}) %collective-permute-start.5) | collective-permute-done | bytes 262176 | tf_op jit(solution)/shard_map/ppermute | solution.py:32
  27.3 1.1 %collective-permute-start.7 = (f32[64,512]{1,0:T(8,128)S(1)}, f32[64,512]{1,0:T(8,128)S(1)}, u32[]{:S(2)}, u32[]{:S(2)}) collective-permute-start(f32[64,512]{1,0:T(8,128)S(1)} %get-tuple-element.77), channel_id=1, source_target_pairs={{0,2},{1,10},{2,18},{3,26},{4,6},{5,14},{6,22},{7,30},{8,3},{9,11}... | collective-permute-start | bytes 393224 | tf_op jit(solution)/shard_map/ppermute | solution.py:233
  28.4 0.7 collective-permute-start.6
  29.0 0.0 copy-done.1
  29.0 1.0 %shard_map.39.ur_ref = bf16[1024,768]{1,0:T(8,128)(2,1)S(1)} custom-call(f32[256,256]{1,0:T(8,128)S(1)} %copy-done.1, f32[8,256,128]{2,1,0:T(8,128)S(1)} %get-tuple-element.62.y_ref), custom_call_target="tpu_custom_call" | custom-call | flops 402653184 | bytes 2097152 | tf_op jit(solution)/shard_map/pallas_call | solution.py:284
  30.1 4.3 %collective-permute-start.9 = (f32[1,64,512]{2,1,0:T(8,128)S(1)}, f32[1,64,512]{2,1,0:T(8,128)S(1)}, u32[]{:S(2)}, u32[]{:S(2)}) collective-permute-start(f32[1,64,512]{2,1,0:T(8,128)S(1)} %constant_dynamic-slice_fusion), channel_id=1, source_target_pairs={{0,16},{8,24},{16,0},{24,8},{1,17},{9,25},{17,1},{25,9},{2,18},{10... | collective-permute-start | bytes 393224 | tf_op jit(solution)/shard_map/ppermute | solution.py:32
  34.4 0.7 collective-permute-start.10
  35.1 0.0 collective-permute-done.7
  35.1 0.0 collective-permute-done.6
  35.1 3.3 %collective-permute-start.8 = (f32[1,32,512]{2,1,0:T(8,128)S(1)}, f32[1,32,512]{2,1,0:T(8,128)S(1)}, u32[]{:S(2)}, u32[]{:S(2)}) collective-permute-start(f32[1,32,512]{2,1,0:T(8,128)S(1)} %get-tuple-element.90), channel_id=1, source_target_pairs={{0,4},{1,5},{2,6},{3,7},{4,0},{5,1},{6,2},{7,3},{8,12},{9,13},{10,... | collective-permute-start | bytes 196616 | tf_op jit(solution)/shard_map/ppermute | solution.py:32
  38.5 0.1 collective-permute-start.15
  38.5 3.7 %collective-permute-done.9 = f32[1,64,512]{2,1,0:T(8,128)S(1)} collective-permute-done((f32[1,64,512]{2,1,0:T(8,128)S(1)}, f32[1,64,512]{2,1,0:T(8,128)S(1)}, u32[]{:S(2)}, u32[]{:S(2)}) %collective-permute-start.9) | collective-permute-done | bytes 131104 | tf_op jit(solution)/shard_map/ppermute | solution.py:32
  42.2 0.0 collective-permute-done.10
  42.3 0.0 collective-permute-done.8
  42.3 4.4 %collective-permute-start.13 = (f32[2,32,512]{2,1,0:T(8,128)S(1)}, f32[2,32,512]{2,1,0:T(8,128)S(1)}, u32[]{:S(2)}, u32[]{:S(2)}) collective-permute-start(f32[2,32,512]{2,1,0:T(8,128)S(1)} %maximum_bitcast_fusion.2.first_ref), channel_id=1, source_target_pairs={{0,2},{1,3},{2,0},{3,1},{4,6},{5,7},{6,4},{7,5},{8,10},{9,11},{10,... | collective-permute-start | bytes 393224 | tf_op jit(solution)/shard_map/ppermute | solution.py:32
  46.8 0.0 collective-permute-done.15
  46.8 0.6 collective-permute-start.16
  47.4 1.3 %collective-permute-start.11 = (f32[1,4,32,512]{3,2,1,0:T(8,128)S(1)}, f32[1,4,32,512]{3,2,1,0:T(8,128)S(1)}, u32[]{:S(2)}, u32[]{:S(2)}) collective-permute-start(f32[1,4,32,512]{3,2,1,0:T(8,128)S(1)} %bitcast.131), channel_id=1, source_target_pairs={{0,16},{8,24},{16,0},{24,8},{1,17},{9,25},{17,1},{25,9},{2,18},{10... | collective-permute-start | bytes 786440 | tf_op jit(solution)/shard_map/ppermute | solution.py:32
  48.8 1.9 %collective-permute-done.13 = f32[2,32,512]{2,1,0:T(8,128)S(1)} collective-permute-done((f32[2,32,512]{2,1,0:T(8,128)S(1)}, f32[2,32,512]{2,1,0:T(8,128)S(1)}, u32[]{:S(2)}, u32[]{:S(2)}) %collective-permute-start.13) | collective-permute-done | bytes 131104 | tf_op jit(solution)/shard_map/ppermute | solution.py:32
  50.7 0.7 shard_map.42
  51.4 0.1 collective-permute-start.18
  51.4 0.2 collective-permute-start.14
  51.6 1.5 %collective-permute-done.16 = f32[2,32,512]{2,1,0:T(8,128)S(1)} collective-permute-done((f32[2,32,512]{2,1,0:T(8,128)S(1)}, f32[2,32,512]{2,1,0:T(8,128)S(1)}, u32[]{:S(2)}, u32[]{:S(2)}) %collective-permute-start.16) | collective-permute-done | bytes 131104 | tf_op jit(solution)/shard_map/ppermute | solution.py:32
  53.2 0.3 collective-permute-start.17
  53.5 0.0 collective-permute-done.18
  53.5 1.4 %collective-permute-start.19 = (f32[32,512]{1,0:T(8,128)S(1)}, f32[32,512]{1,0:T(8,128)S(1)}, u32[]{:S(2)}, u32[]{:S(2)}) collective-permute-start(f32[32,512]{1,0:T(8,128)S(1)} %add.18), channel_id=1, source_target_pairs={{0,16},{8,24},{16,0},{24,8},{1,17},{9,25},{17,1},{25,9},{2,18},{10... | collective-permute-start | bytes 196616 | tf_op jit(solution)/shard_map/ppermute | solution.py:32
  54.9 1.3 %collective-permute-done.11 = f32[1,4,32,512]{3,2,1,0:T(8,128)S(1)} collective-permute-done((f32[1,4,32,512]{3,2,1,0:T(8,128)S(1)}, f32[1,4,32,512]{3,2,1,0:T(8,128)S(1)}, u32[]{:S(2)}, u32[]{:S(2)}) %collective-permute-start.11) | collective-permute-done | bytes 262176 | tf_op jit(solution)/shard_map/ppermute | solution.py:32
  56.3 0.1 collective-permute-start.12
  56.4 1.4 %collective-permute-done.19 = f32[32,512]{1,0:T(8,128)S(1)} collective-permute-done((f32[32,512]{1,0:T(8,128)S(1)}, f32[32,512]{1,0:T(8,128)S(1)}, u32[]{:S(2)}, u32[]{:S(2)}) %collective-permute-start.19) | collective-permute-done | bytes 65568 | tf_op jit(solution)/shard_map/ppermute | solution.py:32
  57.8 1.8 %collective-permute-start.22 = (f32[1,32,512]{2,1,0:T(8,128)S(1)}, f32[1,32,512]{2,1,0:T(8,128)S(1)}, u32[]{:S(2)}, u32[]{:S(2)}) collective-permute-start(f32[1,32,512]{2,1,0:T(8,128)S(1)} %add_bitcast_fusion.refs_0_), channel_id=1, source_target_pairs={{0,3},{1,2},{2,1},{3,0},{4,7},{5,6},{6,5},{7,4},{8,11},{9,10},{10,... | collective-permute-start | bytes 196616 | tf_op jit(solution)/shard_map/ppermute | solution.py:32
  59.7 1.4 %collective-permute-start.21 = (f32[1,32,512]{2,1,0:T(8,128)S(1)}, f32[1,32,512]{2,1,0:T(8,128)S(1)}, u32[]{:S(2)}, u32[]{:S(2)}) collective-permute-start(f32[1,32,512]{2,1,0:T(8,128)S(1)} %add_bitcast_fusion.refs_0_), channel_id=1, source_target_pairs={{0,2},{1,3},{2,0},{3,1},{4,6},{5,7},{6,4},{7,5},{8,10},{9,11},{10,... | collective-permute-start | bytes 196616 | tf_op jit(solution)/shard_map/ppermute | solution.py:32
  61.1 0.0 collective-permute-done.14
  61.1 0.3 collective-permute-start.20
  61.5 0.0 collective-permute-done.12
  61.5 0.1 select_bitcast_fusion.1
  61.6 0.1 pad_maximum_fusion
  61.7 0.4 shard_map.40
  62.2 0.2 collective-permute-done.17.came_ref
  62.4 1.1 %shard_map.41.rest_ref = f32[1024,512]{1,0:T(8,128)S(1)} custom-call(f32[1024,512]{1,0:T(8,128)S(1)} %get-tuple-element.35.a_ref, bf16[768,512]{1,0:T(8,128)(2,1)S(1)} %get-tuple-element.57.uc_ref, f32[8,32,512]{2,1,0:T(8,128)S(1)} %bitcast.123, f32[4,32,512]{2,1,0:T(8,128)S(1)} %bitcast.128, f32[4,32,512]{2,1,0:T(8,128)S(1)} %collective-permute-done.17.came_ref), custom_call_target="tpu_custom_call" | custom-call | flops 805306368 | bytes 4194304 | tf_op jit(solution)/shard_map/pallas_call | solution.py:336
  63.5 0.2 collective-permute-done.22.refs_3_
  63.7 0.8 %collective-permute-done.21.refs_2_ = f32[1,32,512]{2,1,0:T(8,128)S(1)} collective-permute-done((f32[1,32,512]{2,1,0:T(8,128)S(1)}, f32[1,32,512]{2,1,0:T(8,128)S(1)}, u32[]{:S(2)}, u32[]{:S(2)}) %collective-permute-start.21) | collective-permute-done | bytes 65568 | tf_op jit(solution)/shard_map/ppermute | solution.py:32
  64.5 0.9 %collective-permute-done.20.refs_1_ = f32[1,32,512]{2,1,0:T(8,128)S(1)} collective-permute-done((f32[1,32,512]{2,1,0:T(8,128)S(1)}, f32[1,32,512]{2,1,0:T(8,128)S(1)}, u32[]{:S(2)}, u32[]{:S(2)}) %collective-permute-start.20) | collective-permute-done | bytes 65568 | tf_op jit(solution)/shard_map/ppermute | solution.py:32
  65.4 2.2 %shard_map.43 = f32[4096,128]{1,0:T(8,128)} custom-call(f32[1024,512]{1,0:T(8,128)S(1)} %shard_map.41.rest_ref, bf16[1024,768]{1,0:T(8,128)(2,1)S(1)} %shard_map.39.ur_ref, bf16[768,512]{1,0:T(8,128)(2,1)S(1)} %get-tuple-element.57.uc_ref, f32[256,512]{1,0:T(8,128)S(1)} %get-tuple-element.61.zc_ref, f32[1,32,512]{2,1,0:T(8,128)S(1)} %add_bitcast_fusion.refs_0_, ...), custom_call_target="tpu_custom_call" | custom-call | flops 805306368 | bytes 4194304 | tf_op jit(solution)/shard_map/pallas_call | solution.py:347
  (31 shorter events, 0.7 us)
Async XLA Ops:
  0.0 10.5 %collective-permute-start = (f32[1,8,32,128]{3,2,1,0:T(8,128)}, f32[1,8,32,128]{3,2,1,0:T(8,128)S(1)}, u32[]{:S(2)}, u32[]{:S(2)}) collective-permute-start(f32[1,8,32,128]{3,2,1,0:T(8,128)} %bitcast.129), channel_id=1, source_target_pairs={{0,4},{1,5},{2,6},{3,7},{4,0},{5,1},{6,2},{7,3},{8,12},{9,13},{10,... | collective-permute-start | bytes 393224 | tf_op jit(solution)/shard_map/ppermute | solution.py:32
  4.0 1.6 %copy-start = (f32[8,1,128,4,1,128]{5,4,3,2,1,0:T(1,128)S(1)}, f32[8,1,128,4,1,128]{5,4,3,2,1,0:T(1,128)}, u32[]{:S(2)}) copy-start(f32[8,1,128,4,1,128]{5,4,3,2,1,0:T(1,128)} %param.3) | copy-start | bytes 6291460
  5.6 0.9 %copy-start.2 = (f32[8,1,128,32]{2,3,1,0:T(8,128)S(1)}, f32[8,1,128,32]{2,3,1,0:T(8,128)}, u32[]{:S(2)}) copy-start(f32[8,1,128,32]{2,3,1,0:T(8,128)} %param.4) | copy-start | bytes 393220
  10.6 5.0 %collective-permute-start.3 = (f32[2,4,32,128]{3,2,1,0:T(8,128)S(1)}, f32[2,4,32,128]{3,2,1,0:T(8,128)S(1)}, u32[]{:S(2)}, u32[]{:S(2)}) collective-permute-start(f32[2,4,32,128]{3,2,1,0:T(8,128)S(1)} %get-tuple-element.81), channel_id=1, source_target_pairs={{0,1},{1,0},{2,3},{3,2},{4,5},{5,4},{6,7},{7,6},{8,9},{9,8},{10,11... | collective-permute-start | bytes 393224 | tf_op jit(solution)/shard_map/ppermute | solution.py:32
  12.2 5.0 %collective-permute-start.1 = (f32[2,4,32,128]{3,2,1,0:T(8,128)S(1)}, f32[2,4,32,128]{3,2,1,0:T(8,128)S(1)}, u32[]{:S(2)}, u32[]{:S(2)}) collective-permute-start(f32[2,4,32,128]{3,2,1,0:T(8,128)S(1)} %get-tuple-element.82), channel_id=1, source_target_pairs={{0,2},{1,3},{2,0},{3,1},{4,6},{5,7},{6,4},{7,5},{8,10},{9,11},{10,... | collective-permute-start | bytes 393224 | tf_op jit(solution)/shard_map/ppermute | solution.py:32
  15.7 7.1 %collective-permute-start.4 = (f32[4,4,32,128]{3,2,1,0:T(8,128)S(1)}, f32[4,4,32,128]{3,2,1,0:T(8,128)S(1)}, u32[]{:S(2)}, u32[]{:S(2)}) collective-permute-start(f32[4,4,32,128]{3,2,1,0:T(8,128)S(1)} %bitcast.134), channel_id=1, source_target_pairs={{0,2},{1,3},{2,0},{3,1},{4,6},{5,7},{6,4},{7,5},{8,10},{9,11},{10,... | collective-permute-start | bytes 786440 | tf_op jit(solution)/shard_map/ppermute | solution.py:32
  17.3 6.9 %collective-permute-start.2 = (f32[4,4,32,128]{3,2,1,0:T(8,128)S(1)}, f32[4,4,32,128]{3,2,1,0:T(8,128)S(1)}, u32[]{:S(2)}, u32[]{:S(2)}) collective-permute-start(f32[4,4,32,128]{3,2,1,0:T(8,128)S(1)} %bitcast.135), channel_id=1, source_target_pairs={{0,1},{1,0},{2,3},{3,2},{4,5},{5,4},{6,7},{7,6},{8,9},{9,8},{10,11... | collective-permute-start | bytes 786440 | tf_op jit(solution)/shard_map/ppermute | solution.py:32
  24.5 4.5 %copy-start.1 = (f32[256,256]{1,0:T(8,128)S(1)}, f32[256,256]{1,0:T(8,128)}, u32[]{:S(2)}) copy-start(f32[256,256]{1,0:T(8,128)} %t_ref.3) | copy-start | bytes 786436
  25.6 1.6 %collective-permute-start.5 = (f32[2,64,512]{2,1,0:T(8,128)S(1)}, f32[2,64,512]{2,1,0:T(8,128)S(1)}, u32[]{:S(2)}, u32[]{:S(2)}) collective-permute-start(f32[2,64,512]{2,1,0:T(8,128)S(1)} %get-tuple-element.45), channel_id=1, source_target_pairs={{0,8},{8,0},{16,24},{24,16},{1,9},{9,1},{17,25},{25,17},{2,10},{10... | collective-permute-start | bytes 786440 | tf_op jit(solution)/shard_map/ppermute | solution.py:32
  27.3 7.8 %collective-permute-start.7 = (f32[64,512]{1,0:T(8,128)S(1)}, f32[64,512]{1,0:T(8,128)S(1)}, u32[]{:S(2)}, u32[]{:S(2)}) collective-permute-start(f32[64,512]{1,0:T(8,128)S(1)} %get-tuple-element.77), channel_id=1, source_target_pairs={{0,2},{1,10},{2,18},{3,26},{4,6},{5,14},{6,22},{7,30},{8,3},{9,11}... | collective-permute-start | bytes 393224 | tf_op jit(solution)/shard_map/ppermute | solution.py:233
  28.4 6.7 %collective-permute-start.6 = (f32[64,512]{1,0:T(8,128)S(1)}, f32[64,512]{1,0:T(8,128)S(1)}, u32[]{:S(2)}, u32[]{:S(2)}) collective-permute-start(f32[64,512]{1,0:T(8,128)S(1)} %get-tuple-element.78), channel_id=1, source_target_pairs={{0,0},{1,8},{2,16},{3,24},{4,4},{5,12},{6,20},{7,28},{8,1},{9,9},{... | collective-permute-start | bytes 393224 | tf_op jit(solution)/shard_map/ppermute | solution.py:233
  30.1 12.1 %collective-permute-start.9 = (f32[1,64,512]{2,1,0:T(8,128)S(1)}, f32[1,64,512]{2,1,0:T(8,128)S(1)}, u32[]{:S(2)}, u32[]{:S(2)}) collective-permute-start(f32[1,64,512]{2,1,0:T(8,128)S(1)} %constant_dynamic-slice_fusion), channel_id=1, source_target_pairs={{0,16},{8,24},{16,0},{24,8},{1,17},{9,25},{17,1},{25,9},{2,18},{10... | collective-permute-start | bytes 393224 | tf_op jit(solution)/shard_map/ppermute | solution.py:32
  34.4 7.8 %collective-permute-start.10 = (f32[64,512]{1,0:T(8,128)S(1)}, f32[64,512]{1,0:T(8,128)S(1)}, u32[]{:S(2)}, u32[]{:S(2)}) collective-permute-start(f32[64,512]{1,0:T(8,128)S(1)} %copy_bitcast_fusion), channel_id=1, source_target_pairs={{0,0},{1,8},{2,16},{3,24},{4,4},{5,12},{6,20},{7,28},{8,1},{9,9},{... | collective-permute-start | bytes 393224 | tf_op jit(solution)/shard_map/ppermute | solution.py:233
  35.1 7.2 %collective-permute-start.8 = (f32[1,32,512]{2,1,0:T(8,128)S(1)}, f32[1,32,512]{2,1,0:T(8,128)S(1)}, u32[]{:S(2)}, u32[]{:S(2)}) collective-permute-start(f32[1,32,512]{2,1,0:T(8,128)S(1)} %get-tuple-element.90), channel_id=1, source_target_pairs={{0,4},{1,5},{2,6},{3,7},{4,0},{5,1},{6,2},{7,3},{8,12},{9,13},{10,... | collective-permute-start | bytes 196616 | tf_op jit(solution)/shard_map/ppermute | solution.py:32
  38.5 8.3 %collective-permute-start.15 = (f32[1,32,512]{2,1,0:T(8,128)S(1)}, f32[1,32,512]{2,1,0:T(8,128)S(1)}, u32[]{:S(2)}, u32[]{:S(2)}) collective-permute-start(f32[1,32,512]{2,1,0:T(8,128)S(1)} %get-tuple-element.89), channel_id=1, source_target_pairs={{0,4},{1,5},{2,6},{3,7},{4,0},{5,1},{6,2},{7,3},{8,12},{9,13},{10,... | collective-permute-start | bytes 196616 | tf_op jit(solution)/shard_map/ppermute | solution.py:32
  42.3 8.3 %collective-permute-start.13 = (f32[2,32,512]{2,1,0:T(8,128)S(1)}, f32[2,32,512]{2,1,0:T(8,128)S(1)}, u32[]{:S(2)}, u32[]{:S(2)}) collective-permute-start(f32[2,32,512]{2,1,0:T(8,128)S(1)} %maximum_bitcast_fusion.2.first_ref), channel_id=1, source_target_pairs={{0,2},{1,3},{2,0},{3,1},{4,6},{5,7},{6,4},{7,5},{8,10},{9,11},{10,... | collective-permute-start | bytes 393224 | tf_op jit(solution)/shard_map/ppermute | solution.py:32
  46.8 6.3 %collective-permute-start.16 = (f32[2,32,512]{2,1,0:T(8,128)S(1)}, f32[2,32,512]{2,1,0:T(8,128)S(1)}, u32[]{:S(2)}, u32[]{:S(2)}) collective-permute-start(f32[2,32,512]{2,1,0:T(8,128)S(1)} %maximum_bitcast_fusion.3.second_ref), channel_id=1, source_target_pairs={{0,1},{1,0},{2,3},{3,2},{4,5},{5,4},{6,7},{7,6},{8,9},{9,8},{10,11... | collective-permute-start | bytes 393224 | tf_op jit(solution)/shard_map/ppermute | solution.py:32
  47.4 8.8 %collective-permute-start.11 = (f32[1,4,32,512]{3,2,1,0:T(8,128)S(1)}, f32[1,4,32,512]{3,2,1,0:T(8,128)S(1)}, u32[]{:S(2)}, u32[]{:S(2)}) collective-permute-start(f32[1,4,32,512]{3,2,1,0:T(8,128)S(1)} %bitcast.131), channel_id=1, source_target_pairs={{0,16},{8,24},{16,0},{24,8},{1,17},{9,25},{17,1},{25,9},{2,18},{10... | collective-permute-start | bytes 786440 | tf_op jit(solution)/shard_map/ppermute | solution.py:32
  51.4 2.1 %collective-permute-start.18 = (f32[32,512]{1,0:T(8,128)S(1)}, f32[32,512]{1,0:T(8,128)S(1)}, u32[]{:S(2)}, u32[]{:S(2)}) collective-permute-start(f32[32,512]{1,0:T(8,128)S(1)} %shard_map.42), channel_id=1, source_target_pairs={{0,8},{8,0},{16,24},{24,16},{1,9},{9,1},{17,25},{25,17},{2,10},{10... | collective-permute-start | bytes 196616 | tf_op jit(solution)/shard_map/ppermute | solution.py:32
  51.4 9.7 %collective-permute-start.14 = (f32[4,32,512]{2,1,0:T(8,128)S(1)}, f32[4,32,512]{2,1,0:T(8,128)S(1)}, u32[]{:S(2)}, u32[]{:S(2)}) collective-permute-start(f32[4,32,512]{2,1,0:T(8,128)S(1)} %bitcast.132), channel_id=1, source_target_pairs={{0,1},{1,0},{2,3},{3,2},{4,5},{5,4},{6,7},{7,6},{8,9},{9,8},{10,11... | collective-permute-start | bytes 786440 | tf_op jit(solution)/shard_map/ppermute | solution.py:32
  53.2 9.2 %collective-permute-start.17 = (f32[4,32,512]{2,1,0:T(8,128)S(1)}, f32[4,32,512]{2,1,0:T(8,128)S(1)}, u32[]{:S(2)}, u32[]{:S(2)}) collective-permute-start(f32[4,32,512]{2,1,0:T(8,128)S(1)} %bitcast.127), channel_id=1, source_target_pairs={{0,2},{1,3},{2,0},{3,1},{4,6},{5,7},{6,4},{7,5},{8,10},{9,11},{10,... | collective-permute-start | bytes 786440 | tf_op jit(solution)/shard_map/ppermute | solution.py:32
  53.5 4.3 %collective-permute-start.19 = (f32[32,512]{1,0:T(8,128)S(1)}, f32[32,512]{1,0:T(8,128)S(1)}, u32[]{:S(2)}, u32[]{:S(2)}) collective-permute-start(f32[32,512]{1,0:T(8,128)S(1)} %add.18), channel_id=1, source_target_pairs={{0,16},{8,24},{16,0},{24,8},{1,17},{9,25},{17,1},{25,9},{2,18},{10... | collective-permute-start | bytes 196616 | tf_op jit(solution)/shard_map/ppermute | solution.py:32
  56.3 5.2 %collective-permute-start.12 = (f32[2,4,32,512]{3,2,1,0:T(8,128)S(1)}, f32[2,4,32,512]{3,2,1,0:T(8,128)S(1)}, u32[]{:S(2)}, u32[]{:S(2)}) collective-permute-start(f32[2,4,32,512]{3,2,1,0:T(8,128)S(1)} %maximum_bitcast_fusion), channel_id=1, source_target_pairs={{0,8},{8,0},{16,24},{24,16},{1,9},{9,1},{17,25},{25,17},{2,10},{10... | collective-permute-start | bytes 1572872 | tf_op jit(solution)/shard_map/ppermute | solution.py:32
  57.8 5.8 %collective-permute-start.22 = (f32[1,32,512]{2,1,0:T(8,128)S(1)}, f32[1,32,512]{2,1,0:T(8,128)S(1)}, u32[]{:S(2)}, u32[]{:S(2)}) collective-permute-start(f32[1,32,512]{2,1,0:T(8,128)S(1)} %add_bitcast_fusion.refs_0_), channel_id=1, source_target_pairs={{0,3},{1,2},{2,1},{3,0},{4,7},{5,6},{6,5},{7,4},{8,11},{9,10},{10,... | collective-permute-start | bytes 196616 | tf_op jit(solution)/shard_map/ppermute | solution.py:32
  59.7 4.8 %collective-permute-start.21 = (f32[1,32,512]{2,1,0:T(8,128)S(1)}, f32[1,32,512]{2,1,0:T(8,128)S(1)}, u32[]{:S(2)}, u32[]{:S(2)}) collective-permute-start(f32[1,32,512]{2,1,0:T(8,128)S(1)} %add_bitcast_fusion.refs_0_), channel_id=1, source_target_pairs={{0,2},{1,3},{2,0},{3,1},{4,6},{5,7},{6,4},{7,5},{8,10},{9,11},{10,... | collective-permute-start | bytes 196616 | tf_op jit(solution)/shard_map/ppermute | solution.py:32
  61.1 4.3 %collective-permute-start.20 = (f32[1,32,512]{2,1,0:T(8,128)S(1)}, f32[1,32,512]{2,1,0:T(8,128)S(1)}, u32[]{:S(2)}, u32[]{:S(2)}) collective-permute-start(f32[1,32,512]{2,1,0:T(8,128)S(1)} %add_bitcast_fusion.refs_0_), channel_id=1, source_target_pairs={{0,1},{1,0},{2,3},{3,2},{4,5},{5,4},{6,7},{7,6},{8,9},{9,8},{10,11... | collective-permute-start | bytes 196616 | tf_op jit(solution)/shard_map/ppermute | solution.py:32
